TPU v7x, 256 devices: a whole 4x4x8 slice. The times are simulated.
256 devices in a mesh: img: 64 (over y, z, core), grp: 4 (over x).
Axes of the slice: x: 4, y: 4, z: 8, core: 2. Of those that a mesh axis runs over, the one named last changes fastest.
Arguments:
- tokens: bfloat16 [256, 96, 1024], P('img'), may hold values from -6 to 6
- embed_weight: bfloat16 [1024, 768], replicated, may hold values from -0.1875 to 0.1875
- gain_query: float32 [768], replicated, may hold values from 0.5 to 9
- gain_memory: float32 [768], replicated, may hold values from 0.5 to 9
- query_weight: bfloat16 [768, 768], replicated, may hold values from -0.5 to 0.5
- key_weight: bfloat16 [768, 768], replicated, may hold values from -0.5 to 0.5
- value_weight: bfloat16 [768, 768], replicated, may hold values from -0.21875 to 0.21875
- out_weight: bfloat16 [768, 768], replicated, may hold values from -0.21875 to 0.21875
- pair_list: int32 [9216, 2], P(('img', 'grp')), may hold values from 0 to 255, as said below
- counts: int32 [256], P(('img', 'grp')), may hold values from 27 to 36, as said below
Outputs:
- decoded: bfloat16 [9216, 96, 768], P(('img', 'grp'))
Inputs may be any that keep to these rules, and one draw needn't show every extreme that they name: `pair_list`: slots p of device d are rows d * 36 to (d + 1) * 36 - 1. The query image of such a slot lies in [(d div 4) * 4, (d div 4 + 1) * 4). The memory images of one device's slots belong to owners (image div 4) that differ from one another and from d div 4. `counts`: some device has all 36 slots live.
All inputs are finite; a program needn't handle non-finite values.
Results may differ from a plain program's by a relative error of at most 0.04.
The roundings to bfloat16 on the way count: a program that leaves them out, or rounds other values in their place, can miss the bound.
Values may be sent and summed in bfloat16 or wider, within the bound.
A program may use at most 192 MiB of HBM per device.

v0:
```python
import jax
import jax.numpy as jnp
from jax import lax
from jax.sharding import PartitionSpec as P

HEADS = 12
HEAD = 64
D_DEC = 768


epsilon = 1e-06


def normalize(values_in, gain_vector):
    values_in = values_in.astype(jnp.float32)
    row_mean = jnp.mean(values_in, axis=-1, keepdims=True)
    centred = values_in - row_mean
    variance = jnp.mean(centred * centred, axis=-1, keepdims=True)
    return centred * lax.rsqrt(variance + epsilon) * gain_vector


def prepare(
    token_rows, embed_weight, gain_query, gain_memory, query_weight, key_weight, value_weight
):
    image_count, length, feature_width = token_rows.shape
    embedded = jnp.dot(
        token_rows.reshape(image_count * length, feature_width),
        embed_weight,
        preferred_element_type=jnp.float32,
    ).astype(jnp.bfloat16)
    query_normed = normalize(embedded, gain_query).astype(jnp.bfloat16)
    memory_normed = normalize(embedded, gain_memory).astype(jnp.bfloat16)
    queries = jnp.dot(query_normed, query_weight, preferred_element_type=jnp.float32).astype(
        jnp.bfloat16
    )
    key_rows = jnp.dot(memory_normed, key_weight, preferred_element_type=jnp.float32).astype(
        jnp.bfloat16
    )
    value_rows = jnp.dot(memory_normed, value_weight, preferred_element_type=jnp.float32).astype(
        jnp.bfloat16
    )
    payload = jnp.concatenate((key_rows, value_rows), axis=1)
    return (
        embedded.reshape(image_count, length, -1),
        queries.reshape(image_count, length, -1),
        payload.reshape(image_count, length, -1),
    )


def attend(query_rows, key_rows, value_rows, base_rows, out_weight, slot_live):
    slot_count = query_rows.shape[0]
    length = query_rows.shape[1]
    split_shape = (slot_count, length, HEADS, HEAD)
    scores = jnp.einsum(
        "sqhd,skhd->shqk",
        query_rows.reshape(split_shape),
        key_rows.reshape(split_shape),
        preferred_element_type=jnp.float32,
    ) * HEAD ** (-0.5)
    weights = jax.nn.softmax(scores, axis=-1).astype(jnp.bfloat16)
    context = jnp.einsum(
        "shqk,skhd->sqhd",
        weights,
        value_rows.reshape(split_shape),
        preferred_element_type=jnp.float32,
    ).astype(jnp.bfloat16)
    projected = jnp.dot(
        context.reshape(slot_count * length, HEADS * HEAD),
        out_weight,
        preferred_element_type=jnp.float32,
    )
    combined = base_rows.astype(jnp.float32) + projected.reshape(slot_count, length, HEADS * HEAD)
    return jnp.where(slot_live[:, None, None], combined, jnp.float32(0.0)).astype(jnp.bfloat16)


def on_device(
    tokens,
    embed_weight,
    gain_query,
    gain_memory,
    query_weight,
    key_weight,
    value_weight,
    out_weight,
    pair_list,
    counts,
):
    images_here = tokens.shape[0]
    owners = lax.axis_size("img")
    share_rows = tokens.shape[1] // lax.axis_size("grp")
    start_row = lax.axis_index("grp") * share_rows
    token_share = lax.dynamic_slice_in_dim(tokens, start_row, share_rows, 1)
    embedded, queries, payload = prepare(
        token_share, embed_weight, gain_query, gain_memory, query_weight, key_weight, value_weight
    )
    embedded, queries, payload = (
        lax.all_gather(embedded, "grp", axis=1, tiled=True),
        lax.all_gather(queries, "grp", axis=1, tiled=True),
        lax.all_gather(payload, "grp", axis=1, tiled=True),
    )
    slot_total = pair_list.shape[0]
    slot_live = jnp.arange(slot_total, dtype=jnp.int32) < counts[0]
    owner_of = pair_list[:, 1] // images_here
    local_of = pair_list[:, 1] % images_here
    matches = (owner_of[:, None] == jnp.arange(owners, dtype=jnp.int32)[None, :]) & slot_live[
        :, None
    ]
    wanted = jnp.sum(jnp.where(matches, local_of[:, None] + 1, 0), axis=0) - 1
    asked_for = lax.all_to_all(
        wanted.reshape(owners, 1), "img", split_axis=0, concat_axis=0, tiled=True
    ).reshape(owners)
    chosen = jnp.take(payload, jnp.maximum(asked_for, 0), axis=0)
    chosen = jnp.where((asked_for >= 0)[:, None, None], chosen, jnp.zeros((), jnp.bfloat16))
    arrived = lax.all_to_all(chosen, "img", split_axis=0, concat_axis=0, tiled=True)
    memory = jnp.take(arrived, owner_of, axis=0)
    key_rows = memory[:, :, :D_DEC]
    value_rows = memory[:, :, D_DEC:]
    query_local = pair_list[:, 0] % images_here
    query_rows = jnp.take(queries, query_local, axis=0)
    base_rows = jnp.take(embedded, query_local, axis=0)
    return attend(query_rows, key_rows, value_rows, base_rows, out_weight, slot_live)


def solution(mesh):
    placed = (
        P("img", None, None),
        P(),
        P(),
        P(),
        P(),
        P(),
        P(),
        P(),
        P(("img", "grp"), None),
        P(("img", "grp")),
    )
    return jax.shard_map(
        on_device,
        mesh=mesh,
        in_specs=placed,
        out_specs=P(("img", "grp"), None, None),
        check_vma=False,
    )
```

profile of v0, /device:TPU:1, one launch (start us, length us, event | category | flops | bytes accessed | tf_op | source)
XLA Modules:
  0.0 588.0 jit_solution(17420208846057203575)
XLA Ops:
  6.5 1.1 constant_dynamic-slice_fusion
  7.6 0.4 copy-done
  8.0 0.5 convert_reduce_fusion
  8.5 0.2 fusion.16
  8.7 1.7 convolution_convert_fusion.1
  10.4 1.7 convolution_convert_fusion.2
  12.1 0.7 pad_maximum_fusion
  13.5 0.7 and_bitcast_fusion
  14.2 0.1 select_reduce_fusion
  14.4 22.2 %all_to_all.11 = s32[64,1,1]{2,1,0:T(1,128)S(1)} all-to-all(s32[64,1,1]{2,1,0:T(1,128)S(1)} %copy.28), channel_id=1, replica_groups=mesh['img'=64,'grp'=4] {'img'}, dimensions={0} | all-to-all | bytes 512 | tf_op jit(solution)/shard_map/all_to_all | solution.py:109
  36.7 1.2 maximum_reduce_fusion
  37.9 2.4 compare_reduce_fusion.1
  40.3 2.5 all-gather.2.cloned.1.call-done
  42.8 9.5 %gather_fusion = bf16[64,96,1536]{2,1,0:T(8,128)(2,1)} fusion(bf16[4,96,1536]{2,1,0:T(8,128)(2,1)} %all-gather.2.cloned.1.call-done, s32[1024]{0:T(1024)S(1)} %pad_clamp_fusion.1), kind=kCustom, calls=%fused_computation.2 | custom fusion | bytes 37748992 | tf_op jit(solution)/shard_map/jit(_take)/gather | solution.py:112
  52.2 17.5 %select_select_fusion = bf16[64,96,1536]{2,1,0:T(8,128)(2,1)} fusion(bf16[64,96,1536]{2,1,0:T(8,128)(2,1)} %gather_fusion, pred[64]{0:T(512)(128)(4,1)S(1)} %get-tuple-element.7, pred[64]{0:T(512)(128)(4,1)S(1)} %get-tuple-element.6), kind=kLoop, calls=%fused_computation.7 | loop fusion | flops 18874368 | bytes 37748864 | tf_op jit(solution)/shard_map/jit(_where)/select_n | solution.py:113
  69.7 12.1 %all-to-all-start.1 = ((bf16[64,96,1536]{2,1,0:T(8,128)(2,1)}), bf16[64,96,1536]{2,1,0:T(8,128)(2,1)}, u32[]{:S(2)}, u32[]{:S(2)}) async-start(bf16[64,96,1536]{2,1,0:T(8,128)(2,1)} %select_select_fusion), calls=%async_computation.1 | async-start | bytes 37748736 | tf_op jit(solution)/shard_map/all_to_all | solution.py:114
  81.9 0.4 convolution_convert_fusion
  82.2 11.2 %all_gather.11 = bf16[4,96,768]{2,1,0:T(8,128)(2,1)S(1)} all-gather(bf16[4,24,768]{2,1,0:T(8,128)(2,1)S(1)} %bitcast.44), channel_id=1, replica_groups=mesh['img'=64,'grp'=4] {'grp'}, dimensions={1}, use_global_device_ids=true | all-gather | bytes 737280 | tf_op jit(solution)/shard_map/all_gather | solution.py:98
  93.5 4.7 gather_fusion.3
  98.2 5.5 broadcast_select_fusion.1
  103.7 8.4 %copy.30 = bf16[36,96,768]{1,2,0:T(8,128)(2,1)} copy(bf16[36,96,768]{2,1,0:T(8,128)(2,1)} %broadcast_select_fusion.1) | data formatting | bytes 10616832 | tf_op jit(solution)/shard_map/jit(_take)/select_n | solution.py:119
  112.0 12.2 %all_gather.9 = bf16[4,96,768]{2,1,0:T(8,128)(2,1)S(1)} all-gather(bf16[4,24,768]{2,1,0:T(8,128)(2,1)S(1)} %bitcast.41), channel_id=1, replica_groups=mesh['img'=64,'grp'=4] {'grp'}, dimensions={1}, use_global_device_ids=true | all-gather | bytes 737280 | tf_op jit(solution)/shard_map/all_gather | solution.py:97
  124.2 4.9 gather_fusion.2
  129.1 363.2 %all-to-all-done.1 = bf16[64,96,1536]{2,1,0:T(8,128)(2,1)} async-done(((bf16[64,96,1536]{2,1,0:T(8,128)(2,1)}), bf16[64,96,1536]{2,1,0:T(8,128)(2,1)}, u32[]{:S(2)}, u32[]{:S(2)}) %all-to-all-start.1) | async-done | bytes 18874400 | tf_op jit(solution)/shard_map/all_to_all | solution.py:114
  492.3 12.2 %gather_fusion.1 = bf16[36,96,1536]{2,1,0:T(8,128)(2,1)} fusion(bf16[64,96,1536]{2,1,0:T(8,128)(2,1)} %all-to-all-done.1, s32[1024]{0:T(1024)S(1)} %pad_clamp_fusion), kind=kCustom, calls=%fused_computation.3 | custom fusion | bytes 21233808 | tf_op jit(solution)/shard_map/jit(_take)/gather | solution.py:115
  504.5 9.6 %broadcast_select_fusion = bf16[36,96,1536]{2,1,0:T(8,128)(2,1)} fusion(bf16[36,96,1536]{2,1,0:T(8,128)(2,1)} %gather_fusion.1, pred[36]{0:T(512)(128)(4,1)S(1)} %get-tuple-element.8), kind=kLoop, calls=%fused_computation.13 | loop fusion | flops 5308416 | bytes 21233700 | tf_op jit(solution)/shard_map/jit(_take)/select_n | solution.py:115
  514.1 8.7 %fusion.29 = (bf16[36,96,768]{2,1,0:T(8,128)(2,1)}, bf16[36,96,768]{2,1,0:T(8,128)(2,1)}) fusion(bf16[36,96,1536]{2,1,0:T(8,128)(2,1)} %broadcast_select_fusion), kind=kLoop, calls=%fused_computation.66 | loop fusion | bytes 21233664 | tf_op jit(solution)/shard_map/slice | solution.py:116
  522.8 8.4 %copy.31 = bf16[36,96,768]{1,2,0:T(8,128)(2,1)} copy(bf16[36,96,768]{2,1,0:T(8,128)(2,1)} %get-tuple-element.13) | data formatting | bytes 10616832 | tf_op jit(solution)/shard_map/slice | solution.py:116
  531.2 8.4 %copy.29 = bf16[36,96,768]{1,2,0:T(8,128)(2,1)} copy(bf16[36,96,768]{2,1,0:T(8,128)(2,1)} %get-tuple-element.14) | data formatting | bytes 10616832 | tf_op jit(solution)/shard_map/slice | solution.py:117
  539.6 15.3 %fusion.30 = (f32[36,12,96]{2,1,0:T(8,128)S(1)}, f32[36,12,96,96]{2,3,1,0:T(8,128)}) fusion(bf16[36,96,12,64]{1,3,2,0:T(8,128)(2,1)} %bitcast.38, bf16[36,96,12,64]{1,3,2,0:T(8,128)(2,1)} %bitcast.39), kind=kOutput, calls=%fused_computation.67 | convolution fusion | flops 521551968 | bytes 26707968 | tf_op jit(solution)/shard_map/sub | solution.py:60
  554.9 13.8 %fusion.6 = bf16[36,12,64,96]{3,2,1,0:T(8,128)(2,1)} fusion(bf16[36,96,12,64]{1,3,2,0:T(8,128)(2,1)} %bitcast.40, f32[36,12,96,96]{2,3,1,0:T(8,128)} %get-tuple-element.18, f32[36,12,96]{2,1,0:T(8,128)S(1)} %get-tuple-element.17), kind=kOutput, calls=%fused_computation.14 | convolution fusion | flops 520224768 | bytes 26707968 | tf_op jit(solution)/shard_map/shqk,skhd->sqhd/dot_general | solution.py:61
  568.7 12.5 %select_convert_fusion = bf16[36,96,768]{2,1,0:T(8,128)(2,1)} fusion(bf16[36,96,768]{2,1,0:T(8,128)(2,1)} %gather_fusion.2, pred[36]{0:T(512)(128)(4,1)S(1)} %get-tuple-element.11, pred[36]{0:T(512)(128)(4,1)S(1)} %iota_compare_fusion.1, bf16[36,96,768]{1,2,0:T(8,128)(2,1)} %bitcast.46, bf16[768,768]{1,0:T(8,128)(2,1)S(1)} %copy-done.5), kind=kOutput, calls=%fused_computation.10 | convolution fusion | flops 4090134528 | bytes 17104968 | tf_op jit(solution)/shard_map/dot_general | solution.py:67
  (24 shorter events, 0.2 us)
Async XLA Ops:
  6.5 1.5 copy-start
  6.5 36.2 %all-gather.2.cloned.1.call-start = ((), (), s32[]{:S(2)}) async-start(), calls=%async_computation.2 | async-start | bytes 1474560 | tf_op jit(solution)/shard_map/all_gather | solution.py:99
  69.7 12.1 %copy-start.4 = (s32[36,2]{0,1:T(2,128)S(1)}, s32[36,2]{0,1:T(2,128)}, u32[]{:S(2)}) copy-start(s32[36,2]{0,1:T(2,128)} %param.20) | copy-start | bytes 868
  69.7 12.1 %copy-start.2 = (bf16[768,768]{1,0:T(8,128)(2,1)S(1)}, bf16[768,768]{1,0:T(8,128)(2,1)}, u32[]{:S(2)}) copy-start(bf16[768,768]{1,0:T(8,128)(2,1)} %param.16) | copy-start | bytes 3538948
  69.7 12.1 %copy-start.3 = (f32[768]{0:T(1024)S(1)}, f32[768]{0:T(1024)}, u32[]{:S(2)}) copy-start(f32[768]{0:T(1024)} %param.14) | copy-start | bytes 9220
  69.7 422.6 %all-to-all-start.1 = ((bf16[64,96,1536]{2,1,0:T(8,128)(2,1)}), bf16[64,96,1536]{2,1,0:T(8,128)(2,1)}, u32[]{:S(2)}, u32[]{:S(2)}) async-start(bf16[64,96,1536]{2,1,0:T(8,128)(2,1)} %select_select_fusion), calls=%async_computation.1 | async-start | bytes 37748736 | tf_op jit(solution)/shard_map/all_to_all | solution.py:114
  554.9 13.8 %copy-start.5 = (bf16[768,768]{1,0:T(8,128)(2,1)S(1)}, bf16[768,768]{1,0:T(8,128)(2,1)}, u32[]{:S(2)}) copy-start(bf16[768,768]{1,0:T(8,128)(2,1)} %param.19) | copy-start | bytes 3538948
  568.7 12.5 %copy-start.1 = (bf16[1024,768]{1,0:T(8,128)(2,1)S(1)}, bf16[1024,768]{1,0:T(8,128)(2,1)}, u32[]{:S(2)}) copy-start(bf16[1024,768]{1,0:T(8,128)(2,1)} %param.13) | copy-start | bytes 4718596
Sparse Core Ops, SparseCore 0:
  13.0 29.7 all-gather.1
where the time goes:
time: 589 us; the launch traced here: 588 us
  waiting for transfers between devices  366 us (62%)
  local copies, waits for them, and re-layouts  66.7 us (11%)
  matrix products  45.7 us (8%)
  blocking collectives  45.6 us (8%)
  other arithmetic  38 us (6%)
  between operations  14.2 us (2%)
  starting transfers between devices  12.1 us (2%)
    all_to_all x1, waiting for transfers between devices, on_device(): lax.all_to_all(chosen, 'img', split_axis=0, concat_axis=0, tiled=True)  363 us
    all_to_all x1, blocking collectives, on_device(): lax.all_to_all(wanted.reshape(owners, 1), 'img', split_axis=0, concat_axi...  22.2 us
    select_n x1, other arithmetic, on_device(): jnp.where((asked_for >= 0)[:, None, None], chosen, jnp.zeros((), jnp.bflo...  17.5 us
    slice x2, local copies, waits for them, and re-layouts, on_device(): key_rows = memory[:, :, :D_DEC]  17.1 us
    sub x1, matrix products, attend(): weights = jax.nn.softmax(scores, axis=-1).astype(jnp.bfloat16)  15.3 us
    dot_general x1, matrix products, attend(): jnp.einsum('shqk,skhd->sqhd', weights, value_rows.reshape(split_shape), p...  13.8 us
    dot_general x1, matrix products, attend(): jnp.dot(context.reshape(slot_count * length, HEADS * HEAD), out_weight, p...  12.5 us
    gather x1, local copies, waits for them, and re-layouts, on_device(): memory = jnp.take(arrived, owner_of, axis=0)  12.2 us
  transfers between devices with their start and end apart: 2, of which 2 were waited for; matrix products, arithmetic and copies ran while one was open for 5% of the time, Pallas kernels for 0%

commit v1 on v0

v1 whole, which is shorter than its diff:
```python
import functools

import jax
import jax.numpy as jnp
from jax import lax
from jax.experimental import pallas as pl
from jax.experimental.pallas import tpu as pltpu
from jax.sharding import PartitionSpec as P

HEADS = 12
HEAD = 64
D_DEC = 768
D_ENC = 1024
TOK = 96
IMG = 4
SLOTS = 36
EPS = 1e-06

QR = TOK // 2
QC = D_DEC // 2
CH = 3
CR = QR // CH
KINDS = (2, 2, 1)
GROUP = 12

NY, NZ, NX = 4, 8, 4
MESH = pl.DeviceIdType.MESH
BF = jnp.bfloat16
F32 = jnp.float32


def build_messages():
    messages = []

    def add(name, link, size, after, **where):
        messages.append(dict(name=name, link=link, size=size, after=tuple(after), **where))

    for k in range(CH):
        quads = KINDS[k]
        hz, hy = NZ // 2, NY // 2
        az, by = [], []
        for s in range(1, hz + 1):
            for d in (1, -1):
                half = s == hz
                name = ("az", k, d, s)
                images = (0, 2) if not half else ((0, 1) if d == 1 else (1, 1))
                add(name, ("z", d), quads * images[1], [("az", k, d, s - 1)] if s > 1 else [("own", k)],
                    k=k, y=("one", 0), z=("one", -d * (s - 1)), l=images, quads=quads)
                az.append(name)
        for s in range(1, hy + 1):
            for d in (1, -1):
                half = s == hy
                name = ("by", k, d, s)
                images = (2, 2) if not half else ((2, 1) if d == 1 else (3, 1))
                add(name, ("y", d), quads * images[1], [("by", k, d, s - 1)] if s > 1 else [("own", k)],
                    k=k, y=("one", -d * (s - 1)), z=("one", 0), l=images, quads=quads)
                by.append(name)
        for s in range(1, hy + 1):
            for d in (1, -1):
                half = s == hy
                images = (0, 2) if not half else ((0, 1) if d == 1 else (1, 1))
                add(("ay", k, d, s), ("y", d), quads * images[1] * NZ, [("ay", k, d, s - 1)] if s > 1 else az,
                    k=k, y=("one", -d * (s - 1)), z=("all",), l=images, quads=quads)
        for s in range(1, hz + 1):
            for d in (1, -1):
                half = s == hz
                images = (2, 2) if not half else ((2, 1) if d == 1 else (3, 1))
                add(("bz", k, d, s), ("z", d), quads * images[1] * NY, [("bz", k, d, s - 1)] if s > 1 else by,
                    k=k, y=("all",), z=("one", -d * (s - 1)), l=images, quads=quads)
        add(("sa", k, 0), ("c", 1), quads * 2 * NZ, az, k=k, y=("one", 0), z=("all",), l=(0, 2), quads=quads)
        for s in range(1, hy):
            for d in (1, -1):
                add(("sa", k, d * s), ("c", 1), quads * 2 * NZ, [("ay", k, d, s)],
                    k=k, y=("one", -d * s), z=("all",), l=(0, 2), quads=quads)
        add(("sa", k, hy), ("c", 1), quads * 2 * NZ, [("ay", k, 1, hy), ("ay", k, -1, hy)],
            k=k, y=("one", hy), z=("all",), l=(0, 2), quads=quads)
        add(("sb", k, 0), ("c", 1), quads * 2 * NY, by, k=k, y=("all",), z=("one", 0), l=(2, 2), quads=quads)
        for s in range(1, hz):
            for d in (1, -1):
                add(("sb", k, d * s), ("c", 1), quads * 2 * NY, [("bz", k, d, s)],
                    k=k, y=("all",), z=("one", -d * s), l=(2, 2), quads=quads)
        add(("sb", k, hz), ("c", 1), quads * 2 * NY, [("bz", k, 1, hz), ("bz", k, -1, hz)],
            k=k, y=("all",), z=("one", hz), l=(2, 2), quads=quads)
        for g in range(SLOTS // GROUP):
            for d in (1, -1):
                if quads == 1:
                    add(("xf", k, d, g), ("x", d), GROUP // 2, [("sel", k)], k=k, g=g, d=d)
            for d in (1, -1):
                add(("xd", k, d, g), ("x", d), GROUP, [("sel", k)], k=k, g=g, d=d)
            if quads == 1:
                for d in (1, -1):
                    add(("xx", k, d, g), ("x", d), GROUP // 2, [("xf", k, d, g)], k=k, g=g, d=d)
    return messages


def build_order(messages):
    rate = {"x": 0.045, "y": 0.045, "z": 0.045, "c": 0.25}
    unit = CR * QC * 2 / 1e6
    done = set()
    waiting = list(messages)
    flying = []
    free = {}
    now = 0.0
    order = []

    def launch():
        rest = []
        for m in waiting:
            if all(a in done for a in m["after"]):
                start = max(now, free.get(m["link"], 0.0))
                end = start + m["size"] * unit / rate[m["link"][0]]
                free[m["link"]] = end
                flying.append((end + 1.5, len(order), m))
                order.append(("start", m["name"]))
            else:
                rest.append(m)
        waiting[:] = rest

    for k in range(CH):
        order.append(("own", k))
        done.add(("own", k))
    launch()
    need = {k: {m["name"] for m in messages if m["k"] == k and m["name"][0] in ("ay", "bz", "az", "by", "sa", "sb")}
            for k in range(CH)}
    while flying:
        flying.sort(key=lambda f: f[:2])
        t, _, m = flying.pop(0)
        now = max(now, t)
        order.append(("wait", m["name"]))
        done.add(m["name"])
        launch()
        for k in range(CH):
            if need[k] is not None and need[k] <= done:
                need[k] = None
                order.append(("sel", k))
                now += 1.0
                done.add(("sel", k))
                launch()
    assert not waiting
    return order, now


MESSAGES = build_messages()
ORDER, MODELLED = build_order(MESSAGES)
NUMBER = {m["name"]: n for n, m in enumerate(MESSAGES)}


def wrap(value, size):
    return lax.rem(value + 2 * size, size)


def exchange_kernel(tokens_ref, embed_weight_ref, want_ref, embedded_ref, memory_ref, *scratch):
    gathered, (out_going, passing, send_sem, recv_sem) = scratch[:CH], scratch[CH:]
    img = lax.axis_index("img")
    x = lax.axis_index("grp")
    y = img // (2 * NZ)
    z = lax.rem(img // 2, NZ)
    core = lax.rem(img, 2)

    def device(link):
        axis, d = link
        if axis == "x":
            return (img, wrap(x + d, NX))
        if axis == "y":
            return ((wrap(y + d, NY) * NZ + z) * 2 + core, x)
        if axis == "z":
            return ((y * NZ + wrap(z + d, NZ)) * 2 + core, x)
        return ((y * NZ + z) * 2 + (1 - core), x)

    barrier = pltpu.get_barrier_semaphore()
    partners = [("x", 1), ("x", -1), ("y", 1), ("y", -1), ("z", 1), ("z", -1), ("c", 1)]
    for link in partners:
        pl.semaphore_signal(barrier, inc=1, device_id=device(link), device_id_type=MESH)

    for n in range(IMG):
        embedded_ref[n] = jnp.dot(tokens_ref[n], embed_weight_ref[...], preferred_element_type=F32).astype(BF)

    pl.semaphore_wait(barrier, len(partners))

    def slice_of(m):
        def pick(where, at, size):
            return pl.ds(0, size) if where[0] == "all" else pl.ds(wrap(at + where[1], size), 1)

        first, count = m["l"]
        return gathered[m["k"]].at[pl.ds(0, m["quads"]), core, pick(m["y"], y, NY), pick(m["z"], z, NZ),
                           pl.ds(first, count)]

    def descriptor(name):
        n = NUMBER[name]
        m = MESSAGES[n]
        kind = name[0]
        if kind in ("xd", "xf", "xx"):
            k, g, d = m["k"], m["g"], m["d"]
            slots = pl.ds(g * GROUP, GROUP)
            half = GROUP // 2
            first = g * GROUP + (0 if d == 1 else half)
            if kind == "xd":
                src = out_going.at[k, 0 if d == 1 else 1, slots]
                dst = memory_ref.at[(-d) % NX, k, slots]
            elif kind == "xf":
                src = out_going.at[k, 2, pl.ds(first, half)]
                dst = passing.at[k, pl.ds(first, half)]
            else:
                src = passing.at[k, pl.ds(first, half)]
                dst = memory_ref.at[2, k, pl.ds(first, half)]
        else:
            src = dst = slice_of(m)
        return pltpu.make_async_remote_copy(
            src_ref=src, dst_ref=dst, send_sem=send_sem.at[n], recv_sem=recv_sem.at[n],
            device_id=device(m["link"]), device_id_type=MESH)

    def place_own(k):
        for q in range(KINDS[k]):
            quadrant = wrap(x + 2 * q, 4)
            row = pl.multiple_of((quadrant // 2) * QR + k * CR, CR)
            column = pl.multiple_of(lax.rem(quadrant, 2) * QC, 128)
            for n in range(IMG):
                gathered[k][q, core, y, z, n] = embedded_ref[n, pl.ds(row, CR), pl.ds(column, QC)]

    def select(k):
        def body(s, carry):
            def read(q, d):
                image = want_ref[wrap(x + d, NX), s]
                owner = image // IMG
                return gathered[k][q, lax.rem(owner, 2), owner // (2 * NZ), lax.rem(owner // 2, NZ),
                                   lax.rem(image, IMG)]

            out_going[k, 0, s] = read(0, 1)
            out_going[k, 1, s] = read(0, -1)
            if KINDS[k] == 1:
                out_going[k, 2, s] = read(0, 2)
            else:
                memory_ref[2, k, s] = read(1, 0)
            memory_ref[0, k, s] = read(0, 0)
            return carry

        lax.fori_loop(0, SLOTS, body, 0)

    for what, which in ORDER:
        if what == "own":
            place_own(which)
        elif what == "sel":
            select(which)
        elif what == "start":
            descriptor(which).start()
        else:
            descriptor(which).wait_recv()
    for m in MESSAGES:
        descriptor(m["name"]).wait_send()


def exchange(tokens, embed_weight, want):
    vmem = pl.BlockSpec(memory_space=pltpu.VMEM)
    return pl.pallas_call(
        exchange_kernel,
        out_shape=(
            jax.ShapeDtypeStruct((IMG, TOK, D_DEC), BF),
            jax.ShapeDtypeStruct((4, CH, SLOTS, CR, QC), BF),
        ),
        in_specs=[vmem, vmem, pl.BlockSpec(memory_space=pltpu.SMEM)],
        out_specs=(vmem, vmem),
        scratch_shapes=[
            *(pltpu.VMEM((quads, 2, NY, NZ, IMG, CR, QC), BF) for quads in KINDS),
            pltpu.VMEM((CH, 3, SLOTS, CR, QC), BF),
            pltpu.VMEM((CH, SLOTS, CR, QC), BF),
            pltpu.SemaphoreType.DMA((len(MESSAGES),)),
            pltpu.SemaphoreType.DMA((len(MESSAGES),)),
        ],
        compiler_params=pltpu.CompilerParams(
            collective_id=0, has_side_effects=True, vmem_limit_bytes=56 * 1024 * 1024
        ),
        name="exchange",
    )(tokens, embed_weight, want)


def normed(rows, gain):
    rows = rows.astype(F32)
    centred = rows - jnp.mean(rows, axis=-1, keepdims=True)
    variance = jnp.mean(centred * centred, axis=-1, keepdims=True)
    return (centred * lax.rsqrt(variance + EPS) * gain).astype(BF)


PAIRS_OF_HEADS = HEADS // 2
BATCH = 3


def decode_kernel(query_ref, count_ref, memory_ref, embedded_ref, query_weight_ref, key_weight_ref, value_weight_ref,
                  out_weight_ref, gain_query_ref, gain_memory_ref, decoded_ref, stacked, rows, context):
    step = pl.program_id(0)
    x = lax.axis_index("grp")
    lane = lax.broadcasted_iota(jnp.int32, (TOK, 2 * HEAD), 1)

    @pl.when(step == 0)
    def _():
        for n in range(IMG):
            query_rows = jnp.dot(normed(embedded_ref[n], gain_query_ref[...]), query_weight_ref[...],
                                 preferred_element_type=F32).astype(BF).astype(F32) * HEAD ** (-0.5)
            for p in range(PAIRS_OF_HEADS):
                both = query_rows[:, p * 2 * HEAD:(p + 1) * 2 * HEAD]
                stacked[n, p, :TOK] = jnp.where(lane < HEAD, both, 0.0).astype(BF)
                stacked[n, p, TOK:] = jnp.where(lane >= HEAD, both, 0.0).astype(BF)

    for b in range(BATCH):
        for quadrant in range(4):
            relative = wrap(quadrant - x, 4)
            for k in range(CH):
                row = b * TOK + (quadrant // 2) * QR + k * CR
                column = (quadrant % 2) * QC
                rows[row:row + CR, column:column + QC] = memory_ref[relative, k, b]
    memory_normed = normed(rows[...], gain_memory_ref[...])
    keys = jnp.dot(memory_normed, key_weight_ref[...], preferred_element_type=F32).astype(BF)
    values = jnp.dot(memory_normed, value_weight_ref[...], preferred_element_type=F32).astype(BF)
    for b in range(BATCH):
        image = query_ref[step * BATCH + b]
        for p in range(PAIRS_OF_HEADS):
            columns = slice(p * 2 * HEAD, (p + 1) * 2 * HEAD)
            key_pair = keys[b * TOK:(b + 1) * TOK, columns]
            value_pair = values[b * TOK:(b + 1) * TOK, columns]
            scores = lax.dot_general(stacked[image, p], key_pair, (((1,), (1,)), ((), ())),
                                     preferred_element_type=F32)
            weights = jnp.exp(scores - jnp.max(scores, axis=-1, keepdims=True))
            weights = (weights / jnp.sum(weights, axis=-1, keepdims=True)).astype(BF)
            mixed = jnp.dot(weights, value_pair, preferred_element_type=F32)
            context[b * TOK:(b + 1) * TOK, columns] = jnp.where(
                lane < HEAD, mixed[:TOK], mixed[TOK:]).astype(BF)
    projected = jnp.dot(context[...], out_weight_ref[...], preferred_element_type=F32)
    for b in range(BATCH):
        slot = step * BATCH + b
        combined = embedded_ref[query_ref[slot]].astype(F32) + projected[b * TOK:(b + 1) * TOK]
        decoded_ref[b] = jnp.where(slot < count_ref[0], combined, 0.0).astype(BF)


def decode(query_local, counts, memory, embedded, query_weight, key_weight, value_weight, out_weight, gain_query,
           gain_memory):
    def whole(*shape):
        return pl.BlockSpec(shape, lambda i, *_: (0,) * len(shape))

    return pl.pallas_call(
        decode_kernel,
        out_shape=jax.ShapeDtypeStruct((SLOTS, TOK, D_DEC), BF),
        grid_spec=pltpu.PrefetchScalarGridSpec(
            num_scalar_prefetch=2,
            grid=(SLOTS // BATCH,),
            in_specs=[
                pl.BlockSpec((4, CH, BATCH, CR, QC), lambda i, *_: (0, 0, i, 0, 0)),
                whole(IMG, TOK, D_DEC),
                whole(D_DEC, D_DEC),
                whole(D_DEC, D_DEC),
                whole(D_DEC, D_DEC),
                whole(D_DEC, D_DEC),
                whole(1, D_DEC),
                whole(1, D_DEC),
            ],
            out_specs=pl.BlockSpec((BATCH, TOK, D_DEC), lambda i, *_: (i, 0, 0)),
            scratch_shapes=[
                pltpu.VMEM((IMG, PAIRS_OF_HEADS, 2 * TOK, 2 * HEAD), BF),
                pltpu.VMEM((BATCH * TOK, D_DEC), BF),
                pltpu.VMEM((BATCH * TOK, D_DEC), BF),
            ],
        ),
        compiler_params=pltpu.CompilerParams(vmem_limit_bytes=48 * 1024 * 1024),
        name="decode",
    )(query_local, counts, memory, embedded, query_weight, key_weight, value_weight, out_weight,
      gain_query.reshape(1, -1), gain_memory.reshape(1, -1))


def on_device(
    tokens,
    embed_weight,
    gain_query,
    gain_memory,
    query_weight,
    key_weight,
    value_weight,
    out_weight,
    pair_list,
    counts,
):
    want = lax.all_gather(pair_list[:, 1], "grp", axis=0)
    embedded, memory = exchange(tokens, embed_weight, want)
    query_local = lax.rem(pair_list[:, 0], IMG)
    return decode(query_local, counts, memory, embedded, query_weight, key_weight, value_weight, out_weight,
                  gain_query, gain_memory)


def solution(mesh):
    placed = (
        P("img", None, None),
        P(),
        P(),
        P(),
        P(),
        P(),
        P(),
        P(),
        P(("img", "grp"), None),
        P(("img", "grp")),
    )
    return jax.shard_map(
        on_device,
        mesh=mesh,
        in_specs=placed,
        out_specs=P(("img", "grp"), None, None),
        check_vma=False,
    )
```

time: 589 us -> 167 us (0.28)
  waiting for transfers between devices: 366 us -> 0 us
  Pallas kernels: 0 us -> 150 us
  local copies, waits for them, and re-layouts: 66.7 us -> 6.92 us
  matrix products: 45.7 us -> 0 us
  blocking collectives: 45.6 us -> 7.69 us
  other arithmetic: 38 us -> 0.85 us
  between operations: 14.2 us -> 1.35 us
  starting transfers between devices: 12.1 us -> 0 us
    all_to_all x1 -> x0, waiting for transfers between devices: 363 us -> none  [on_device(): lax.all_to_all(chosen, 'img', split_axis=0, concat_axis=0, tiled=True)]
    pallas_call x0 -> x2, Pallas kernels: none -> 150 us  [the longest x1 116 us: exchange(): pl.pallas_call(exchange_kernel, out_shape=(jax.ShapeDtypeStruct((IMG, TOK...]
    select_n x4 -> x0, other arithmetic: 32.6 us -> none  [the longest x1 17.5 us: on_device(): jnp.where((asked_for >= 0)[:, None, None], chosen, jnp.zeros((), jnp.bflo...]
    gather x4 -> x0, local copies, waits for them, and re-layouts: 31.3 us -> none  [the longest x1 12.2 us: on_device(): memory = jnp.take(arrived, owner_of, axis=0)]
    dot_general x6 -> x0, matrix products: 30.4 us -> none  [the longest x1 13.8 us: attend(): jnp.einsum('shqk,skhd->sqhd', weights, value_rows.reshape(split_shape), p...]
    slice x3 -> x0, local copies, waits for them, and re-layouts: 25.4 us -> none  [the longest x2 17.1 us: on_device(): key_rows = memory[:, :, :D_DEC]]
    all_gather x2 -> x0, blocking collectives: 23.4 us -> none  [the longest x1 12.2 us: on_device(): lax.all_gather(embedded, 'grp', axis=1, tiled=True)]
    all_to_all x1 -> x0, blocking collectives: 22.2 us -> none  [on_device(): lax.all_to_all(wanted.reshape(owners, 1), 'img', split_axis=0, concat_axi...]
  transfers between devices with their start and end apart: 2 -> 0, of which waited for: 2 -> 0; matrix products, arithmetic and copies ran while one was open for 5% -> 0% of each run, Pallas kernels for 0% -> 0%
where the time goes in v1:
time: 167 us
  Pallas kernels  150 us (90%)
  blocking collectives  7.69 us (5%)
  local copies, waits for them, and re-layouts  6.92 us (4%)
    pallas_call x1, Pallas kernels, exchange(): pl.pallas_call(exchange_kernel, out_shape=(jax.ShapeDtypeStruct((IMG, TOK...  116 us
    pallas_call x1, Pallas kernels, decode(): pl.pallas_call(decode_kernel, out_shape=jax.ShapeDtypeStruct((SLOTS, TOK,...  34.2 us
    unnamed x1, blocking collectives  7.69 us
    unnamed x12, local copies, waits for them, and re-layouts  4.88 us

profile of v1, /device:TPU:1, one launch (start us, length us, event | category | flops | bytes accessed | tf_op | source)
XLA Modules:
  0.0 166.6 jit_solution(11377736804996503421)
XLA Ops:
  0.7 1.3 dynamic-slice
  2.6 0.9 bitcast_dynamic-update-slice_fusion
  3.4 7.7 %all-reduce = s32[144]{0:T(256)S(1)} all-reduce(s32[144]{0:T(256)S(1)} %get-tuple-element.9), channel_id=2, replica_groups=mesh['img'=64,'grp'=4] {'grp'}, use_global_device_ids=true, to_apply=%add | all-reduce | flops 144 | bytes 1152
  11.1 0.7 reshape.8.want_ref
  11.8 0.7 reshape.6.gain_query_ref
  12.5 0.7 reshape.7.gain_memory_ref
  13.2 0.0 copy-start
  13.2 0.0 copy-start.1
  13.2 115.6 %exchange.1 = (bf16[4,96,768]{2,1,0:T(8,128)(2,1)}, bf16[4,3,36,16,384]{4,3,2,1,0:T(8,128)(2,1)}) custom-call(bf16[4,96,1024]{2,1,0:T(8,128)(2,1)} %tokens_ref.1, bf16[1024,768]{1,0:T(8,128)(2,1)} %embed_weight_ref.1, s32[4,36]{1,0:T(4,128)} %reshape.8.want_ref), custom_call_target="tpu_custom_call" | custom-call | tf_op jit(solution)/shard_map/exchange/pallas_call | solution.py:254
  128.8 0.0 copy-done
  128.8 0.0 copy-done.1
  128.8 0.0 copy-start.2
  128.8 1.3 copy-done.2
  130.1 0.0 copy-start.3
  130.1 1.3 copy-done.3
  131.3 0.0 copy-start.4
  131.3 1.1 copy-done.4
  132.4 34.2 %decode.1 = bf16[36,96,768]{2,1,0:T(8,128)(2,1)} custom-call(s32[36]{0:T(128)S(1)} %get-tuple-element.10.query_ref, s32[1]{0:T(128)S(6)} %copy.12.count_ref, bf16[4,3,36,16,384]{4,3,2,1,0:T(8,128)(2,1)} %get-tuple-element.7.memory_ref, bf16[4,96,768]{2,1,0:T(8,128)(2,1)S(1)} %copy-done.4, bf16[768,768]{1,0:T(8,128)(2,1)S(1)} %copy-done, ...), custom_call_target="tpu_custom_call" | custom-call | tf_op jit(solution)/shard_map/decode/pallas_call | solution.py:338
  (1 shorter events, 0.0 us)
Async XLA Ops:
  13.2 115.6 %copy-start = (bf16[768,768]{1,0:T(8,128)(2,1)S(1)}, bf16[768,768]{1,0:T(8,128)(2,1)}, u32[]{:S(2)}) copy-start(bf16[768,768]{1,0:T(8,128)(2,1)} %query_weight_ref.1) | copy-start | bytes 3538948
  13.2 115.6 %copy-start.1 = (bf16[768,768]{1,0:T(8,128)(2,1)S(1)}, bf16[768,768]{1,0:T(8,128)(2,1)}, u32[]{:S(2)}) copy-start(bf16[768,768]{1,0:T(8,128)(2,1)} %key_weight_ref.1) | copy-start | bytes 3538948
  128.8 1.3 copy-start.2
  130.1 1.3 copy-start.3
  131.3 1.1 copy-start.4

commit v2 on v1

--- a/solution.py
+++ b/solution.py
@@ -20,7 +20,7 @@
 QC = D_DEC // 2
 CH = 3
 CR = QR // CH
-KINDS = (2, 2, 1)
+KINDS = (1, 2, 2)
 GROUP = 12
 
 NY, NZ, NX = 4, 8, 4
@@ -33,82 +33,82 @@
     messages = []
 
     def add(name, link, size, after, **where):
-        messages.append(dict(name=name, link=link, size=size, after=tuple(after), **where))
+        messages.append(dict(name=name, link=link, size=size, after=tuple(after), k=name[1], **where))
+
+    hz, hy = NZ // 2, NY // 2
+
+    def part(first, far, d):
+        return (first, 2) if not far else (first + (d == -1), 1)
 
     for k in range(CH):
         quads = KINDS[k]
-        hz, hy = NZ // 2, NY // 2
-        az, by = [], []
+        own = ("own", k)
+        along_z, along_y = {0: [own]}, {0: [own]}
         for s in range(1, hz + 1):
             for d in (1, -1):
-                half = s == hz
-                name = ("az", k, d, s)
-                images = (0, 2) if not half else ((0, 1) if d == 1 else (1, 1))
-                add(name, ("z", d), quads * images[1], [("az", k, d, s - 1)] if s > 1 else [("own", k)],
-                    k=k, y=("one", 0), z=("one", -d * (s - 1)), l=images, quads=quads)
-                az.append(name)
+                name, images = ("az", k, d, s), part(0, s == hz, d)
+                add(name, ("z", d), quads * images[1], [("az", k, d, s - 1)] if s > 1 else [own],
+                    y=("one", 0), z=("one", -d * (s - 1)), l=images)
+                along_z.setdefault(hz if s == hz else -d * s, []).append(name)
         for s in range(1, hy + 1):
             for d in (1, -1):
-                half = s == hy
-                name = ("by", k, d, s)
-                images = (2, 2) if not half else ((2, 1) if d == 1 else (3, 1))
-                add(name, ("y", d), quads * images[1], [("by", k, d, s - 1)] if s > 1 else [("own", k)],
-                    k=k, y=("one", -d * (s - 1)), z=("one", 0), l=images, quads=quads)
-                by.append(name)
+                name, images = ("by", k, d, s), part(2, s == hy, d)
+                add(name, ("y", d), quads * images[1], [("by", k, d, s - 1)] if s > 1 else [own],
+                    y=("one", -d * (s - 1)), z=("one", 0), l=images)
+                along_y.setdefault(hy if s == hy else -d * s, []).append(name)
+        columns, planes = {}, {}
         for s in range(1, hy + 1):
             for d in (1, -1):
-                half = s == hy
-                images = (0, 2) if not half else ((0, 1) if d == 1 else (1, 1))
-                add(("ay", k, d, s), ("y", d), quads * images[1] * NZ, [("ay", k, d, s - 1)] if s > 1 else az,
-                    k=k, y=("one", -d * (s - 1)), z=("all",), l=images, quads=quads)
+                images = part(0, s == hy, d)
+                for at, arrived in along_z.items():
+                    name = ("ay", k, d, s, at)
+                    add(name, ("y", d), quads * images[1], [("ay", k, d, s - 1, at)] if s > 1 else arrived,
+                        y=("one", -d * (s - 1)), z=("one", at), l=images)
+                    columns.setdefault(hy if s == hy else -d * s, []).append(name)
         for s in range(1, hz + 1):
             for d in (1, -1):
-                half = s == hz
-                images = (2, 2) if not half else ((2, 1) if d == 1 else (3, 1))
-                add(("bz", k, d, s), ("z", d), quads * images[1] * NY, [("bz", k, d, s - 1)] if s > 1 else by,
-                    k=k, y=("all",), z=("one", -d * (s - 1)), l=images, quads=quads)
-        add(("sa", k, 0), ("c", 1), quads * 2 * NZ, az, k=k, y=("one", 0), z=("all",), l=(0, 2), quads=quads)
-        for s in range(1, hy):
-            for d in (1, -1):
-                add(("sa", k, d * s), ("c", 1), quads * 2 * NZ, [("ay", k, d, s)],
-                    k=k, y=("one", -d * s), z=("all",), l=(0, 2), quads=quads)
-        add(("sa", k, hy), ("c", 1), quads * 2 * NZ, [("ay", k, 1, hy), ("ay", k, -1, hy)],
-            k=k, y=("one", hy), z=("all",), l=(0, 2), quads=quads)
-        add(("sb", k, 0), ("c", 1), quads * 2 * NY, by, k=k, y=("all",), z=("one", 0), l=(2, 2), quads=quads)
-        for s in range(1, hz):
-            for d in (1, -1):
-                add(("sb", k, d * s), ("c", 1), quads * 2 * NY, [("bz", k, d, s)],
-                    k=k, y=("all",), z=("one", -d * s), l=(2, 2), quads=quads)
-        add(("sb", k, hz), ("c", 1), quads * 2 * NY, [("bz", k, 1, hz), ("bz", k, -1, hz)],
-            k=k, y=("all",), z=("one", hz), l=(2, 2), quads=quads)
+                images = part(2, s == hz, d)
+                for at, arrived in along_y.items():
+                    name = ("bz", k, d, s, at)
+                    add(name, ("z", d), quads * images[1], [("bz", k, d, s - 1, at)] if s > 1 else arrived,
+                        y=("one", at), z=("one", -d * (s - 1)), l=images)
+                    planes.setdefault(hz if s == hz else -d * s, []).append(name)
+        columns[0] = [n for at in along_z.values() for n in at]
+        planes[0] = [n for at in along_y.values() for n in at]
+        for at, arrived in columns.items():
+            add(("sa", k, at), ("c", 1), quads * 2 * NZ, arrived, y=("one", at), z=("all",), l=(0, 2))
+        for at, arrived in planes.items():
+            add(("sb", k, at), ("c", 1), quads * 2 * NY, arrived, y=("all",), z=("one", at), l=(2, 2))
         for g in range(SLOTS // GROUP):
             for d in (1, -1):
                 if quads == 1:
-                    add(("xf", k, d, g), ("x", d), GROUP // 2, [("sel", k)], k=k, g=g, d=d)
-            for d in (1, -1):
-                add(("xd", k, d, g), ("x", d), GROUP, [("sel", k)], k=k, g=g, d=d)
+                    add(("xf", k, d, g), ("x", d), GROUP // 2, [("sel", k)], g=g, d=d)
+            for d in (1, -1):
+                add(("xd", k, d, g), ("x", d), GROUP, [("sel", k)], g=g, d=d)
             if quads == 1:
                 for d in (1, -1):
-                    add(("xx", k, d, g), ("x", d), GROUP // 2, [("xf", k, d, g)], k=k, g=g, d=d)
+                    add(("xx", k, d, g), ("x", d), GROUP // 2, [("xf", k, d, g)], g=g, d=d)
     return messages
+
+
+LOOK = 1.5
 
 
 def build_order(messages):
     rate = {"x": 0.045, "y": 0.045, "z": 0.045, "c": 0.25}
     unit = CR * QC * 2 / 1e6
-    done = set()
-    waiting = list(messages)
-    flying = []
-    free = {}
-    now = 0.0
-    order = []
+    rank = {"by": 0, "az": 0, "bz": 1, "ay": 1}
+    waiting = sorted(messages, key=lambda m: (m["k"], rank.get(m["name"][0], 2)))
+    done = {("own", k) for k in range(CH)}
+    order = [("own", k) for k in range(CH)]
+    flying, free, now = [], {}, 0.0
 
     def launch():
         rest = []
         for m in waiting:
-            if all(a in done for a in m["after"]):
-                start = max(now, free.get(m["link"], 0.0))
-                end = start + m["size"] * unit / rate[m["link"][0]]
+            at = free.get(m["link"], 0.0)
+            if at - now < LOOK and all(a in done for a in m["after"]):
+                end = max(now, at) + m["size"] * unit / rate[m["link"][0]]
                 free[m["link"]] = end
                 flying.append((end + 1.5, len(order), m))
                 order.append(("start", m["name"]))
@@ -116,16 +116,16 @@
                 rest.append(m)
         waiting[:] = rest
 
-    for k in range(CH):
-        order.append(("own", k))
-        done.add(("own", k))
     launch()
-    need = {k: {m["name"] for m in messages if m["k"] == k and m["name"][0] in ("ay", "bz", "az", "by", "sa", "sb")}
-            for k in range(CH)}
-    while flying:
+    need = {k: {m["name"] for m in messages if m["k"] == k and m["link"][0] != "x"} for k in range(CH)}
+    while flying or waiting:
+        if not flying:
+            now += 0.5
+            launch()
+            continue
         flying.sort(key=lambda f: f[:2])
         t, _, m = flying.pop(0)
-        now = max(now, t)
+        now = max(now, t) + 0.05
         order.append(("wait", m["name"]))
         done.add(m["name"])
         launch()
@@ -136,7 +136,6 @@
                 now += 1.0
                 done.add(("sel", k))
                 launch()
-    assert not waiting
     return order, now
 
 
@@ -182,7 +181,7 @@
             return pl.ds(0, size) if where[0] == "all" else pl.ds(wrap(at + where[1], size), 1)
 
         first, count = m["l"]
-        return gathered[m["k"]].at[pl.ds(0, m["quads"]), core, pick(m["y"], y, NY), pick(m["z"], z, NZ),
+        return gathered[m["k"]].at[pl.ds(0, KINDS[m["k"]]), core, pick(m["y"], y, NY), pick(m["z"], z, NZ),
                            pl.ds(first, count)]
 
     def descriptor(name):

time: 167 us -> 150 us (0.90)
  Pallas kernels: 150 us -> 131 us
    pallas_call x1, Pallas kernels: 116 us -> 97.2 us  [exchange(): pl.pallas_call(exchange_kernel, out_shape=(jax.ShapeDtypeStruct((IMG, TOK...]
where the time goes in v2:
time: 150 us; the launch traced here: 148 us
  Pallas kernels  131 us (87%)
  blocking collectives  7.69 us (5%)
  local copies, waits for them, and re-layouts  6.92 us (5%)
    pallas_call x1, Pallas kernels, exchange(): pl.pallas_call(exchange_kernel, out_shape=(jax.ShapeDtypeStruct((IMG, TOK...  97.2 us
    pallas_call x1, Pallas kernels, decode(): pl.pallas_call(decode_kernel, out_shape=jax.ShapeDtypeStruct((SLOTS, TOK,...  34.2 us
    unnamed x1, blocking collectives  7.69 us
    unnamed x12, local copies, waits for them, and re-layouts  4.88 us

profile of v2, /device:TPU:1, one launch (start us, length us, event | category | flops | bytes accessed | tf_op | source)
XLA Modules:
  0.0 148.2 jit_solution(3609367017125015036)
XLA Ops:
  0.7 1.3 dynamic-slice
  2.6 0.9 bitcast_dynamic-update-slice_fusion
  3.4 7.7 %all-reduce = s32[144]{0:T(256)S(1)} all-reduce(s32[144]{0:T(256)S(1)} %get-tuple-element.9), channel_id=2, replica_groups=mesh['img'=64,'grp'=4] {'grp'}, use_global_device_ids=true, to_apply=%add | all-reduce | flops 144 | bytes 1152
  11.1 0.7 reshape.8.want_ref
  11.8 0.7 reshape.6.gain_query_ref
  12.5 0.7 reshape.7.gain_memory_ref
  13.2 0.0 copy-start
  13.2 0.0 copy-start.1
  13.2 97.2 %exchange.1 = (bf16[4,96,768]{2,1,0:T(8,128)(2,1)}, bf16[4,3,36,16,384]{4,3,2,1,0:T(8,128)(2,1)}) custom-call(bf16[4,96,1024]{2,1,0:T(8,128)(2,1)} %tokens_ref.1, bf16[1024,768]{1,0:T(8,128)(2,1)} %embed_weight_ref.1, s32[4,36]{1,0:T(4,128)} %reshape.8.want_ref), custom_call_target="tpu_custom_call" | custom-call | tf_op jit(solution)/shard_map/exchange/pallas_call | solution.py:253
  110.3 0.0 copy-done
  110.3 0.0 copy-done.1
  110.4 0.0 copy-start.2
  110.4 1.3 copy-done.2
  111.6 0.0 copy-start.3
  111.6 1.3 copy-done.3
  112.9 0.0 copy-start.4
  112.9 1.1 copy-done.4
  114.0 34.2 %decode.1 = bf16[36,96,768]{2,1,0:T(8,128)(2,1)} custom-call(s32[36]{0:T(128)S(1)} %get-tuple-element.10.query_ref, s32[1]{0:T(128)S(6)} %copy.12.count_ref, bf16[4,3,36,16,384]{4,3,2,1,0:T(8,128)(2,1)} %get-tuple-element.7.memory_ref, bf16[4,96,768]{2,1,0:T(8,128)(2,1)S(1)} %copy-done.4, bf16[768,768]{1,0:T(8,128)(2,1)S(1)} %copy-done, ...), custom_call_target="tpu_custom_call" | custom-call | tf_op jit(solution)/shard_map/decode/pallas_call | solution.py:337
  (1 shorter events, 0.0 us)
Async XLA Ops:
  13.2 97.2 %copy-start = (bf16[768,768]{1,0:T(8,128)(2,1)S(1)}, bf16[768,768]{1,0:T(8,128)(2,1)}, u32[]{:S(2)}) copy-start(bf16[768,768]{1,0:T(8,128)(2,1)} %query_weight_ref.1) | copy-start | bytes 3538948
  13.2 97.2 %copy-start.1 = (bf16[768,768]{1,0:T(8,128)(2,1)S(1)}, bf16[768,768]{1,0:T(8,128)(2,1)}, u32[]{:S(2)}) copy-start(bf16[768,768]{1,0:T(8,128)(2,1)} %key_weight_ref.1) | copy-start | bytes 3538948
  110.4 1.3 copy-start.2
  111.6 1.3 copy-start.3
  112.9 1.1 copy-start.4

commit v3 on v2

v3 whole, which is shorter than its diff:
```python
import functools

import jax
import jax.numpy as jnp
from jax import lax
from jax.experimental import pallas as pl
from jax.experimental.pallas import tpu as pltpu
from jax.sharding import PartitionSpec as P

HEADS = 12
HEAD = 64
D_DEC = 768
D_ENC = 1024
TOK = 96
IMG = 4
SLOTS = 36
EPS = 1e-06

QR = TOK // 2
QC = D_DEC // 2
CH = 3
CR = QR // CH
KINDS = (1, 2, 2)
GROUP = 12

NY, NZ, NX = 4, 8, 4
MESH = pl.DeviceIdType.MESH
BF = jnp.bfloat16
F32 = jnp.float32


def build_messages():
    messages = []
    for d in (1, -1, 2):
        messages.append(dict(name=("wt", 0, d), link=("x", d), size=0.5, after=(), k=0, d=d))

    def add(name, link, size, after, **where):
        messages.append(dict(name=name, link=link, size=size, after=tuple(after), k=name[1], **where))

    hz, hy = NZ // 2, NY // 2

    def part(first, far, d):
        return (first, 2) if not far else (first + (d == -1), 1)

    for k in range(CH):
        quads = KINDS[k]
        own = ("own", k)
        along_z, along_y = {0: [own]}, {0: [own]}
        for s in range(1, hz + 1):
            for d in (1, -1):
                name, images = ("az", k, d, s), part(0, s == hz, d)
                add(name, ("z", d), quads * images[1], [("az", k, d, s - 1)] if s > 1 else [own],
                    y=("one", 0), z=("one", -d * (s - 1)), l=images)
                along_z.setdefault(hz if s == hz else -d * s, []).append(name)
        for s in range(1, hy + 1):
            for d in (1, -1):
                name, images = ("by", k, d, s), part(2, s == hy, d)
                add(name, ("y", d), quads * images[1], [("by", k, d, s - 1)] if s > 1 else [own],
                    y=("one", -d * (s - 1)), z=("one", 0), l=images)
                along_y.setdefault(hy if s == hy else -d * s, []).append(name)
        columns, planes = {}, {}
        for s in range(1, hy + 1):
            for d in (1, -1):
                images = part(0, s == hy, d)
                for at, arrived in along_z.items():
                    name = ("ay", k, d, s, at)
                    add(name, ("y", d), quads * images[1], [("ay", k, d, s - 1, at)] if s > 1 else arrived,
                        y=("one", -d * (s - 1)), z=("one", at), l=images)
                    columns.setdefault(hy if s == hy else -d * s, []).append(name)
        for s in range(1, hz + 1):
            for d in (1, -1):
                images = part(2, s == hz, d)
                for at, arrived in along_y.items():
                    name = ("bz", k, d, s, at)
                    add(name, ("z", d), quads * images[1], [("bz", k, d, s - 1, at)] if s > 1 else arrived,
                        y=("one", at), z=("one", -d * (s - 1)), l=images)
                    planes.setdefault(hz if s == hz else -d * s, []).append(name)
        columns[0] = [n for at in along_z.values() for n in at]
        planes[0] = [n for at in along_y.values() for n in at]
        for at, arrived in columns.items():
            add(("sa", k, at), ("c", 1), quads * 2 * NZ, arrived, y=("one", at), z=("all",), l=(0, 2))
        for at, arrived in planes.items():
            add(("sb", k, at), ("c", 1), quads * 2 * NY, arrived, y=("all",), z=("one", at), l=(2, 2))
        for g in range(SLOTS // GROUP):
            for d in (1, -1):
                if quads == 1:
                    add(("xf", k, d, g), ("x", d), GROUP // 2, [("sel", k)], g=g, d=d)
            for d in (1, -1):
                add(("xd", k, d, g), ("x", d), GROUP, [("sel", k)], g=g, d=d)
            if quads == 1:
                for d in (1, -1):
                    add(("xx", k, d, g), ("x", d), GROUP // 2, [("xf", k, d, g)], g=g, d=d)
    return messages


LOOK = 2.0
COST = {"sel": 1.0, "queries": 2.0, "kv": 1.6, "attend": 7.0, "want": 1.0}


def build_order(messages):
    rate = {"x": 0.045, "y": 0.045, "z": 0.045, "c": 0.25}
    unit = CR * QC * 2 / 1e6
    rank = {"wt": -1, "by": 0, "az": 0, "bz": 1, "ay": 1}
    waiting = sorted(messages, key=lambda m: (m["k"], rank.get(m["name"][0], 2)))
    done = {("own", k) for k in range(CH)}
    order = [("own", k) for k in range(CH)]
    flying, free, now = [], {}, 0.0
    groups = range(SLOTS // GROUP)
    steps = [(("want",), {("wt", 0, d) for d in (1, -1, 2)})]
    for k in range(CH):
        gather = {m["name"] for m in messages if m["k"] == k and m["link"][0] != "x"}
        steps.append((("sel", k), gather | {("want",)}))
    steps.append((("queries",), set()))
    for k in range(CH):
        for g in groups:
            here = {m["name"] for m in messages if m["k"] == k and m.get("g") == g and m["name"][0] in ("xd", "xx")}
            steps.append((("kv", k, g), here | {("sel", k)}))
    for g in groups:
        steps.append((("attend", g), {("kv", k, g) for k in range(CH)} | {("queries",)}))

    def launch():
        rest = []
        for m in waiting:
            at = free.get(m["link"], 0.0)
            if at - now < LOOK and all(a in done for a in m["after"]):
                end = max(now, at) + m["size"] * unit / rate[m["link"][0]]
                free[m["link"]] = end
                flying.append((end + 1.5, len(order), m))
                order.append(("start", m["name"]))
            else:
                rest.append(m)
        waiting[:] = rest

    launch()
    while flying or waiting or steps:
        flying.sort(key=lambda f: f[:2])
        ready = [step for step in steps if step[1] <= done]
        if ready and (ready[0][0][0] in ("sel", "want") or not flying or flying[0][0] > now + 0.3):
            name = ready[0][0]
            steps.remove(ready[0])
            order.append(name)
            now += COST[name[0]]
            done.add(name)
        elif flying:
            t, _, m = flying.pop(0)
            now = max(now, t) + 0.05
            order.append(("wait", m["name"]))
            done.add(m["name"])
        else:
            now += 0.5
        launch()
    return order, now


MESSAGES = build_messages()
ORDER, MODELLED = build_order(MESSAGES)
NUMBER = {m["name"]: n for n, m in enumerate(MESSAGES)}


def wrap(value, size):
    return lax.rem(value + 2 * size, size)


def normed(rows, gain):
    rows = rows.astype(F32)
    centred = rows - jnp.mean(rows, axis=-1, keepdims=True)
    variance = jnp.mean(centred * centred, axis=-1, keepdims=True)
    return (centred * lax.rsqrt(variance + EPS) * gain).astype(BF)


PAIRS_OF_HEADS = HEADS // 2
BATCH = 3


def decode_kernel(tokens_ref, embed_weight_ref, gain_query_ref, gain_memory_ref, query_weight_hbm, key_weight_hbm,
                  value_weight_hbm, out_weight_hbm, pairs_ref, count_ref, decoded_hbm, *scratch):
    gathered = scratch[:CH]
    (out_going, passing, memory, embedded, want_vmem, want, weights_vmem, stacked, rows, keys, values, context,
     send_sem, recv_sem, local_sem) = scratch[CH:]
    img = lax.axis_index("img")
    x = lax.axis_index("grp")
    y = img // (2 * NZ)
    z = lax.rem(img // 2, NZ)
    core = lax.rem(img, 2)

    def device(link):
        axis, d = link
        if axis == "x":
            return (img, wrap(x + d, NX))
        if axis == "y":
            return ((wrap(y + d, NY) * NZ + z) * 2 + core, x)
        if axis == "z":
            return ((y * NZ + wrap(z + d, NZ)) * 2 + core, x)
        return ((y * NZ + z) * 2 + (1 - core), x)

    barrier = pltpu.get_barrier_semaphore()
    partners = [("x", 1), ("x", -1), ("x", 2), ("y", 1), ("y", -1), ("z", 1), ("z", -1), ("c", 1)]
    for link in partners:
        pl.semaphore_signal(barrier, inc=1, device_id=device(link), device_id_type=MESH)

    loads = [pltpu.make_async_copy(hbm, weights_vmem.at[n], local_sem.at[n])
             for n, hbm in enumerate((query_weight_hbm, key_weight_hbm, value_weight_hbm, out_weight_hbm))]
    for load in loads:
        load.start()

    want_vmem[0] = jnp.zeros_like(want_vmem[0])
    want_vmem[0, :SLOTS, :2] = pairs_ref[...]
    for n in range(IMG):
        embedded[n] = jnp.dot(tokens_ref[n], embed_weight_ref[...], preferred_element_type=F32).astype(BF)

    pl.semaphore_wait(barrier, len(partners))

    def slice_of(m):
        def pick(where, at, size):
            return pl.ds(0, size) if where[0] == "all" else pl.ds(wrap(at + where[1], size), 1)

        first, count = m["l"]
        return gathered[m["k"]].at[pl.ds(0, KINDS[m["k"]]), core, pick(m["y"], y, NY), pick(m["z"], z, NZ),
                                   pl.ds(first, count)]

    def descriptor(name):
        n = NUMBER[name]
        m = MESSAGES[n]
        kind = name[0]
        half = GROUP // 2
        if kind == "wt":
            src = want_vmem.at[0]
            dst = want_vmem.at[(-m["d"]) % NX]
        elif kind in ("xd", "xf", "xx"):
            k, g, d = m["k"], m["g"], m["d"]
            slots = pl.ds(g * GROUP, GROUP)
            some = pl.ds(g * GROUP + (0 if d == 1 else half), half)
            if kind == "xd":
                src = out_going.at[k, 0 if d == 1 else 1, slots]
                dst = memory.at[(-d) % NX, k, slots]
            elif kind == "xf":
                src = out_going.at[k, 2, some]
                dst = passing.at[k, some]
            else:
                src = passing.at[k, some]
                dst = memory.at[2, k, some]
        else:
            src = dst = slice_of(m)
        return pltpu.make_async_remote_copy(
            src_ref=src, dst_ref=dst, send_sem=send_sem.at[n], recv_sem=recv_sem.at[n],
            device_id=device(m["link"]), device_id_type=MESH)

    def place_own(k):
        for q in range(KINDS[k]):
            quadrant = wrap(x + 2 * q, 4)
            row = pl.multiple_of((quadrant // 2) * QR + k * CR, CR)
            column = pl.multiple_of(lax.rem(quadrant, 2) * QC, 128)
            for n in range(IMG):
                gathered[k][q, core, y, z, n] = embedded[n, pl.ds(row, CR), pl.ds(column, QC)]

    def read_wants():
        move = pltpu.make_async_copy(want_vmem, want, local_sem.at[4])
        move.start()
        move.wait()

    def select(k):
        def body(s, carry):
            def read(q, d):
                image = want[d % NX, s, 1]
                owner = image // IMG
                return gathered[k][q, lax.rem(owner, 2), owner // (2 * NZ), lax.rem(owner // 2, NZ),
                                   lax.rem(image, IMG)]

            out_going[k, 0, s] = read(0, 1)
            out_going[k, 1, s] = read(0, -1)
            if KINDS[k] == 1:
                out_going[k, 2, s] = read(0, 2)
            else:
                memory[2, k, s] = read(1, 0)
            memory[0, k, s] = read(0, 0)
            return carry

        lax.fori_loop(0, SLOTS, body, 0)

    lane = lax.broadcasted_iota(jnp.int32, (TOK, 2 * HEAD), 1)

    def make_queries():
        for load in loads:
            load.wait()

        def body(n, carry):
            query_rows = jnp.dot(normed(embedded[n], gain_query_ref[...]), weights_vmem[0],
                                 preferred_element_type=F32).astype(BF).astype(F32) * HEAD ** (-0.5)
            for p in range(PAIRS_OF_HEADS):
                both = query_rows[:, p * 2 * HEAD:(p + 1) * 2 * HEAD]
                stacked[n, p, :TOK] = jnp.where(lane < HEAD, both, 0.0).astype(BF)
                stacked[n, p, TOK:] = jnp.where(lane >= HEAD, both, 0.0).astype(BF)
            return carry

        lax.fori_loop(0, IMG, body, 0)

    def project(k, g):
        slots = pl.ds(g * GROUP, GROUP)
        for quadrant in range(4):
            part = memory[wrap(quadrant - x, 4), k, slots]
            rows[:, (quadrant // 2) * CR:(quadrant // 2 + 1) * CR, (quadrant % 2) * QC:(quadrant % 2 + 1) * QC] = part
        here = normed(rows[...].reshape(GROUP * 2 * CR, D_DEC), gain_memory_ref[...])
        for n, result in ((1, keys), (2, values)):
            made = jnp.dot(here, weights_vmem[n], preferred_element_type=F32).astype(BF)
            result[slots, 2 * CR * k:2 * CR * (k + 1)] = made.reshape(GROUP, 2 * CR, D_DEC)

    def attend(g):
        def body(i, carry):
            first = g * GROUP + i * BATCH
            for b in range(BATCH):
                slot = first + b
                image = lax.rem(want[0, slot, 0], IMG)
                for p in range(PAIRS_OF_HEADS):
                    columns = slice(p * 2 * HEAD, (p + 1) * 2 * HEAD)
                    scores = lax.dot_general(stacked[image, p], keys[slot, :, columns], (((1,), (1,)), ((), ())),
                                             preferred_element_type=F32)
                    powers = jnp.exp(scores - jnp.max(scores, axis=-1, keepdims=True))
                    share = 1.0 / jnp.sum(powers, axis=-1, keepdims=True)
                    mixed = jnp.dot((powers * share).astype(BF), values[slot, :, columns],
                                    preferred_element_type=F32)
                    context[b * TOK:(b + 1) * TOK, columns] = jnp.where(
                        lane < HEAD, mixed[:TOK], mixed[TOK:]).astype(BF)
            projected = jnp.dot(context[...], weights_vmem[3], preferred_element_type=F32)
            for b in range(BATCH):
                slot = first + b
                image = lax.rem(want[0, slot, 0], IMG)
                combined = embedded[image].astype(F32) + projected[b * TOK:(b + 1) * TOK]
                keys[slot] = jnp.where(slot < count_ref[0], combined, 0.0).astype(BF)
            return carry

        lax.fori_loop(0, GROUP // BATCH, body, 0)
        result(g).start()

    def result(g):
        slots = pl.ds(g * GROUP, GROUP)
        return pltpu.make_async_copy(keys.at[slots], decoded_hbm.at[slots], local_sem.at[5 + g])

    run = dict(own=place_own, want=read_wants, sel=select, queries=make_queries, kv=project, attend=attend,
               start=lambda name: descriptor(name).start(), wait=lambda name: descriptor(name).wait_recv())
    for what, *which in ORDER:
        run[what](*which)
    for m in MESSAGES:
        descriptor(m["name"]).wait_send()
    for g in range(SLOTS // GROUP):
        result(g).wait()


def decode(tokens, embed_weight, gain_query, gain_memory, query_weight, key_weight, value_weight, out_weight, pairs,
           counts):
    vmem = pl.BlockSpec(memory_space=pltpu.VMEM)
    hbm = pl.BlockSpec(memory_space=pl.ANY)
    return pl.pallas_call(
        decode_kernel,
        out_shape=jax.ShapeDtypeStruct((SLOTS, TOK, D_DEC), BF),
        in_specs=[vmem, vmem, vmem, vmem, hbm, hbm, hbm, hbm, vmem, pl.BlockSpec(memory_space=pltpu.SMEM)],
        out_specs=hbm,
        scratch_shapes=[
            *(pltpu.VMEM((quads, 2, NY, NZ, IMG, CR, QC), BF) for quads in KINDS),
            pltpu.VMEM((CH, 3, SLOTS, CR, QC), BF),
            pltpu.VMEM((CH, SLOTS, CR, QC), BF),
            pltpu.VMEM((4, CH, SLOTS, CR, QC), BF),
            pltpu.VMEM((IMG, TOK, D_DEC), BF),
            pltpu.VMEM((NX, 40, 128), jnp.int32),
            pltpu.SMEM((NX, 40, 128), jnp.int32),
            pltpu.VMEM((4, D_DEC, D_DEC), BF),
            pltpu.VMEM((IMG, PAIRS_OF_HEADS, 2 * TOK, 2 * HEAD), BF),
            pltpu.VMEM((GROUP, 2 * CR, D_DEC), BF),
            pltpu.VMEM((SLOTS, TOK, D_DEC), BF),
            pltpu.VMEM((SLOTS, TOK, D_DEC), BF),
            pltpu.VMEM((BATCH * TOK, D_DEC), BF),
            pltpu.SemaphoreType.DMA((len(MESSAGES),)),
            pltpu.SemaphoreType.DMA((len(MESSAGES),)),
            pltpu.SemaphoreType.DMA((5 + SLOTS // GROUP,)),
        ],
        compiler_params=pltpu.CompilerParams(
            collective_id=0, has_side_effects=True, vmem_limit_bytes=60 * 1024 * 1024
        ),
        name="decode",
    )(tokens, embed_weight, gain_query, gain_memory, query_weight, key_weight, value_weight, out_weight, pairs, counts)


def on_device(
    tokens,
    embed_weight,
    gain_query,
    gain_memory,
    query_weight,
    key_weight,
    value_weight,
    out_weight,
    pair_list,
    counts,
):
    return decode(tokens, embed_weight, gain_query, gain_memory, query_weight, key_weight, value_weight, out_weight,
                  pair_list, counts)


def solution(mesh):
    placed = (
        P("img", None, None),
        P(),
        P(),
        P(),
        P(),
        P(),
        P(),
        P(),
        P(("img", "grp"), None),
        P(("img", "grp")),
    )
    return jax.shard_map(
        on_device,
        mesh=mesh,
        in_specs=placed,
        out_specs=P(("img", "grp"), None, None),
        check_vma=False,
    )
```

time: 150 us -> 124 us (0.83)
  Pallas kernels: 131 us -> 116 us
  blocking collectives: 7.69 us -> 0 us
    pallas_call x1 -> x0, Pallas kernels: 97.2 us -> none  [exchange(): pl.pallas_call(exchange_kernel, out_shape=(jax.ShapeDtypeStruct((IMG, TOK...]
    pallas_call x1, Pallas kernels: 34.2 us -> 116 us  [decode(): pl.pallas_call(decode_kernel, out_shape=jax.ShapeDtypeStruct((SLOTS, TOK,...]
    unnamed x1 -> x0, blocking collectives: 7.69 us -> none
    unnamed x12 -> x2, local copies, waits for them, and re-layouts: 4.88 us -> 6.6 us
where the time goes in v3:
time: 124 us; the launch traced here: 123 us
  Pallas kernels  116 us (94%)
  local copies, waits for them, and re-layouts  6.6 us (5%)
    pallas_call x1, Pallas kernels, decode(): pl.pallas_call(decode_kernel, out_shape=jax.ShapeDtypeStruct((SLOTS, TOK,...  116 us
    unnamed x2, local copies, waits for them, and re-layouts  6.6 us

profile of v3, /device:TPU:1, one launch (start us, length us, event | category | flops | bytes accessed | tf_op | source)
XLA Modules:
  0.0 123.4 jit_solution(12188655923483852326)
XLA Ops:
  0.7 1.4 %copy.11.pairs_ref = s32[36,2]{1,0:T(8,128)} copy(s32[36,2]{0,1:T(2,128)} %param.18) | data formatting | bytes 576 | tf_op args[8]
  2.0 116.2 %decode.1 = bf16[36,96,768]{2,1,0:T(8,128)(2,1)} custom-call(bf16[4,96,1024]{2,1,0:T(8,128)(2,1)} %tokens_ref.1, bf16[1024,768]{1,0:T(8,128)(2,1)} %embed_weight_ref.1, f32[768]{0:T(1024)} %gain_query_ref.1, f32[768]{0:T(1024)} %gain_memory_ref.1, bf16[768,768]{1,0:T(8,128)(2,1)} %query_weight_hbm.1, bf16[768,768]{1,0:T(8,128)(2,1)} %key_weight_hbm.1, ...), custom_call_target="tpu_custom_call" | custom-call | tf_op jit(solution)/shard_map/decode/pallas_call | solution.py:352
  118.2 5.2 %copy.14 = bf16[36,96,768]{2,1,0:T(8,128)(2,1)} copy(bf16[36,96,768]{2,1,0:T(8,128)(2,1)} %decode.1) | data formatting | bytes 10616832

commit v4 on v3

--- a/solution.py
+++ b/solution.py
@@ -111,21 +111,22 @@
         gather = {m["name"] for m in messages if m["k"] == k and m["link"][0] != "x"}
         steps.append((("sel", k), gather | {("want",)}))
     steps.append((("queries",), set()))
-    for k in range(CH):
+    last = CH - 1
+    for k in range(last):
         for g in groups:
             here = {m["name"] for m in messages if m["k"] == k and m.get("g") == g and m["name"][0] in ("xd", "xx")}
             steps.append((("kv", k, g), here | {("sel", k)}))
-    for g in groups:
-        steps.append((("attend", g), {("kv", k, g) for k in range(CH)} | {("queries",)}))
+    final = {m["name"] for m in messages if m["k"] == last and m["name"][0] == "xd"}
 
     def launch():
         rest = []
         for m in waiting:
             at = free.get(m["link"], 0.0)
-            if at - now < LOOK and all(a in done for a in m["after"]):
+            if (at - now < LOOK or m["link"][0] == "x") and all(a in done for a in m["after"]):
                 end = max(now, at) + m["size"] * unit / rate[m["link"][0]]
                 free[m["link"]] = end
-                flying.append((end + 1.5, len(order), m))
+                if m["name"] not in final:
+                    flying.append((end + 1.5, len(order), m))
                 order.append(("start", m["name"]))
             else:
                 rest.append(m)
@@ -149,12 +150,14 @@
         else:
             now += 0.5
         launch()
-    return order, now
+    order.append(("finish", [("xd", last, d, 0) for d in (1, -1)]))
+    return order, now + sum(COST[c] for c in ("kv", "attend")) * len(groups)
 
 
 MESSAGES = build_messages()
 ORDER, MODELLED = build_order(MESSAGES)
 NUMBER = {m["name"]: n for n, m in enumerate(MESSAGES)}
+PER_GROUP = [6 if quads == 1 else 2 for quads in KINDS]
 
 
 def wrap(value, size):
@@ -169,11 +172,10 @@
 
 
 PAIRS_OF_HEADS = HEADS // 2
-BATCH = 3
 
 
 def decode_kernel(tokens_ref, embed_weight_ref, gain_query_ref, gain_memory_ref, query_weight_hbm, key_weight_hbm,
-                  value_weight_hbm, out_weight_hbm, pairs_ref, count_ref, decoded_hbm, *scratch):
+                  value_weight_hbm, out_weight_hbm, pairs_ref, count_ref, decoded_ref, *scratch):
     gathered = scratch[:CH]
     (out_going, passing, memory, embedded, want_vmem, want, weights_vmem, stacked, rows, keys, values, context,
      send_sem, recv_sem, local_sem) = scratch[CH:]
@@ -204,7 +206,7 @@
         load.start()
 
     want_vmem[0] = jnp.zeros_like(want_vmem[0])
-    want_vmem[0, :SLOTS, :2] = pairs_ref[...]
+    want_vmem[0, :2, :SLOTS] = pairs_ref[...]
     for n in range(IMG):
         embedded[n] = jnp.dot(tokens_ref[n], embed_weight_ref[...], preferred_element_type=F32).astype(BF)
 
@@ -218,7 +220,7 @@
         return gathered[m["k"]].at[pl.ds(0, KINDS[m["k"]]), core, pick(m["y"], y, NY), pick(m["z"], z, NZ),
                                    pl.ds(first, count)]
 
-    def descriptor(name):
+    def descriptor(name, step=0):
         n = NUMBER[name]
         m = MESSAGES[n]
         kind = name[0]
@@ -227,7 +229,8 @@
             src = want_vmem.at[0]
             dst = want_vmem.at[(-m["d"]) % NX]
         elif kind in ("xd", "xf", "xx"):
-            k, g, d = m["k"], m["g"], m["d"]
+            k, g, d = m["k"], m["g"] + step, m["d"]
+            n = n + step * PER_GROUP[k]
             slots = pl.ds(g * GROUP, GROUP)
             some = pl.ds(g * GROUP + (0 if d == 1 else half), half)
             if kind == "xd":
@@ -235,9 +238,9 @@
                 dst = memory.at[(-d) % NX, k, slots]
             elif kind == "xf":
                 src = out_going.at[k, 2, some]
-                dst = passing.at[k, some]
+                dst = passing.at[some]
             else:
-                src = passing.at[k, some]
+                src = passing.at[some]
                 dst = memory.at[2, k, some]
         else:
             src = dst = slice_of(m)
@@ -261,7 +264,7 @@
     def select(k):
         def body(s, carry):
             def read(q, d):
-                image = want[d % NX, s, 1]
+                image = want[d % NX, 1, s]
                 owner = image // IMG
                 return gathered[k][q, lax.rem(owner, 2), owner // (2 * NZ), lax.rem(owner // 2, NZ),
                                    lax.rem(image, IMG)]
@@ -305,44 +308,42 @@
             result[slots, 2 * CR * k:2 * CR * (k + 1)] = made.reshape(GROUP, 2 * CR, D_DEC)
 
     def attend(g):
-        def body(i, carry):
-            first = g * GROUP + i * BATCH
-            for b in range(BATCH):
-                slot = first + b
-                image = lax.rem(want[0, slot, 0], IMG)
-                for p in range(PAIRS_OF_HEADS):
-                    columns = slice(p * 2 * HEAD, (p + 1) * 2 * HEAD)
-                    scores = lax.dot_general(stacked[image, p], keys[slot, :, columns], (((1,), (1,)), ((), ())),
-                                             preferred_element_type=F32)
-                    powers = jnp.exp(scores - jnp.max(scores, axis=-1, keepdims=True))
-                    share = 1.0 / jnp.sum(powers, axis=-1, keepdims=True)
-                    mixed = jnp.dot((powers * share).astype(BF), values[slot, :, columns],
-                                    preferred_element_type=F32)
-                    context[b * TOK:(b + 1) * TOK, columns] = jnp.where(
-                        lane < HEAD, mixed[:TOK], mixed[TOK:]).astype(BF)
-            projected = jnp.dot(context[...], weights_vmem[3], preferred_element_type=F32)
-            for b in range(BATCH):
-                slot = first + b
-                image = lax.rem(want[0, slot, 0], IMG)
-                combined = embedded[image].astype(F32) + projected[b * TOK:(b + 1) * TOK]
-                keys[slot] = jnp.where(slot < count_ref[0], combined, 0.0).astype(BF)
+        for b in range(GROUP):
+            slot = g * GROUP + b
+            image = lax.rem(want[0, 0, slot], IMG)
+            for p in range(PAIRS_OF_HEADS):
+                columns = slice(p * 2 * HEAD, (p + 1) * 2 * HEAD)
+                scores = lax.dot_general(stacked[image, p], keys[slot, :, columns], (((1,), (1,)), ((), ())),
+                                         preferred_element_type=F32)
+                powers = jnp.exp(scores - jnp.max(scores, axis=-1, keepdims=True))
+                share = 1.0 / jnp.sum(powers, axis=-1, keepdims=True)
+                mixed = jnp.dot((powers * share).astype(BF), values[slot, :, columns], preferred_element_type=F32)
+                context[b * TOK:(b + 1) * TOK, columns] = jnp.where(
+                    lane < HEAD, mixed[:TOK], mixed[TOK:]).astype(BF)
+        projected = jnp.dot(context[...], weights_vmem[3], preferred_element_type=F32)
+        for b in range(GROUP):
+            slot = g * GROUP + b
+            image = lax.rem(want[0, 0, slot], IMG)
+            combined = embedded[image].astype(F32) + projected[b * TOK:(b + 1) * TOK]
+            decoded_ref[slot] = jnp.where(slot < count_ref[0], combined, 0.0).astype(BF)
+
+    def finish(names):
+        def body(g, carry):
+            for name in names:
+                descriptor(name, g).wait_recv()
+            project(CH - 1, g)
+            attend(g)
             return carry
 
-        lax.fori_loop(0, GROUP // BATCH, body, 0)
-        result(g).start()
-
-    def result(g):
-        slots = pl.ds(g * GROUP, GROUP)
-        return pltpu.make_async_copy(keys.at[slots], decoded_hbm.at[slots], local_sem.at[5 + g])
-
-    run = dict(own=place_own, want=read_wants, sel=select, queries=make_queries, kv=project, attend=attend,
+        lax.fori_loop(0, SLOTS // GROUP, body, 0)
+
+    run = dict(own=place_own, want=read_wants, sel=select, queries=make_queries, kv=project,
+               finish=finish,
                start=lambda name: descriptor(name).start(), wait=lambda name: descriptor(name).wait_recv())
     for what, *which in ORDER:
         run[what](*which)
     for m in MESSAGES:
         descriptor(m["name"]).wait_send()
-    for g in range(SLOTS // GROUP):
-        result(g).wait()
 
 
 def decode(tokens, embed_weight, gain_query, gain_memory, query_weight, key_weight, value_weight, out_weight, pairs,
@@ -351,29 +352,29 @@
     hbm = pl.BlockSpec(memory_space=pl.ANY)
     return pl.pallas_call(
         decode_kernel,
-        out_shape=jax.ShapeDtypeStruct((SLOTS, TOK, D_DEC), BF),
+        out_shape=pltpu.VMEM((SLOTS, TOK, D_DEC), BF),
         in_specs=[vmem, vmem, vmem, vmem, hbm, hbm, hbm, hbm, vmem, pl.BlockSpec(memory_space=pltpu.SMEM)],
-        out_specs=hbm,
+        out_specs=vmem,
         scratch_shapes=[
             *(pltpu.VMEM((quads, 2, NY, NZ, IMG, CR, QC), BF) for quads in KINDS),
             pltpu.VMEM((CH, 3, SLOTS, CR, QC), BF),
-            pltpu.VMEM((CH, SLOTS, CR, QC), BF),
+            pltpu.VMEM((SLOTS, CR, QC), BF),
             pltpu.VMEM((4, CH, SLOTS, CR, QC), BF),
             pltpu.VMEM((IMG, TOK, D_DEC), BF),
-            pltpu.VMEM((NX, 40, 128), jnp.int32),
-            pltpu.SMEM((NX, 40, 128), jnp.int32),
+            pltpu.VMEM((NX, 8, 128), jnp.int32),
+            pltpu.SMEM((NX, 8, 128), jnp.int32),
             pltpu.VMEM((4, D_DEC, D_DEC), BF),
             pltpu.VMEM((IMG, PAIRS_OF_HEADS, 2 * TOK, 2 * HEAD), BF),
             pltpu.VMEM((GROUP, 2 * CR, D_DEC), BF),
             pltpu.VMEM((SLOTS, TOK, D_DEC), BF),
             pltpu.VMEM((SLOTS, TOK, D_DEC), BF),
-            pltpu.VMEM((BATCH * TOK, D_DEC), BF),
+            pltpu.VMEM((GROUP * TOK, D_DEC), BF),
             pltpu.SemaphoreType.DMA((len(MESSAGES),)),
             pltpu.SemaphoreType.DMA((len(MESSAGES),)),
-            pltpu.SemaphoreType.DMA((5 + SLOTS // GROUP,)),
+            pltpu.SemaphoreType.DMA((5,)),
         ],
         compiler_params=pltpu.CompilerParams(
-            collective_id=0, has_side_effects=True, vmem_limit_bytes=60 * 1024 * 1024
+            collective_id=0, has_side_effects=True, vmem_limit_bytes=57 * 1024 * 1024
         ),
         name="decode",
     )(tokens, embed_weight, gain_query, gain_memory, query_weight, key_weight, value_weight, out_weight, pairs, counts)
@@ -392,7 +393,7 @@
     counts,
 ):
     return decode(tokens, embed_weight, gain_query, gain_memory, query_weight, key_weight, value_weight, out_weight,
-                  pair_list, counts)
+                  pair_list.T, counts)
 
 
 def solution(mesh):

time: 124 us -> 110 us (0.89)
  Pallas kernels: 116 us -> 106 us
  local copies, waits for them, and re-layouts: 6.6 us -> 2.38 us
    pallas_call x1, Pallas kernels: 116 us -> 106 us  [decode(): pl.pallas_call(decode_kernel, out_shape=pltpu.VMEM((SLOTS, TOK, D_DEC), B...]
    unnamed x2 -> x1, local copies, waits for them, and re-layouts: 6.6 us -> 2.38 us
where the time goes in v4:
time: 110 us; the launch traced here: 109 us
  Pallas kernels  106 us (96%)
  local copies, waits for them, and re-layouts  2.38 us (2%)
    pallas_call x1, Pallas kernels, decode(): pl.pallas_call(decode_kernel, out_shape=pltpu.VMEM((SLOTS, TOK, D_DEC), B...  106 us
    unnamed x1, local copies, waits for them, and re-layouts  2.38 us

profile of v4, /device:TPU:1, one launch (start us, length us, event | category | flops | bytes accessed | tf_op | source)
XLA Modules:
  0.0 109.4 jit_solution(10714228174090178785)
XLA Ops:
  0.7 106.4 %decode.1 = bf16[36,96,768]{2,1,0:T(8,128)(2,1)S(1)} custom-call(bf16[4,96,1024]{2,1,0:T(8,128)(2,1)} %tokens_ref.1, bf16[1024,768]{1,0:T(8,128)(2,1)} %embed_weight_ref.1, f32[768]{0:T(1024)} %gain_query_ref.1, f32[768]{0:T(1024)} %gain_memory_ref.1, bf16[768,768]{1,0:T(8,128)(2,1)} %query_weight_hbm.1, bf16[768,768]{1,0:T(8,128)(2,1)} %key_weight_hbm.1, ...), custom_call_target="tpu_custom_call" | custom-call | tf_op jit(solution)/shard_map/decode/pallas_call | solution.py:353
  107.1 2.4 %copy.12 = bf16[36,96,768]{2,1,0:T(8,128)(2,1)} copy(bf16[36,96,768]{2,1,0:T(8,128)(2,1)S(1)} %decode.1) | data formatting | bytes 10616832

commit v5 on v4

--- a/solution.py
+++ b/solution.py
@@ -94,7 +94,9 @@
 
 
 LOOK = 2.0
-COST = {"sel": 1.0, "queries": 2.0, "kv": 1.6, "attend": 7.0, "want": 1.0}
+LOOK_X = 2.5
+COST = {"sel": 1.0, "queries": 1.5, "kv": 1.2, "attend": 6.0, "want": 0.5}
+EVENTS = 8
 
 
 def build_order(messages):
@@ -104,7 +106,7 @@
     waiting = sorted(messages, key=lambda m: (m["k"], rank.get(m["name"][0], 2)))
     done = {("own", k) for k in range(CH)}
     order = [("own", k) for k in range(CH)]
-    flying, free, now = [], {}, 0.0
+    flying, free, now, since = [], {}, 0.0, 0
     groups = range(SLOTS // GROUP)
     steps = [(("want",), {("wt", 0, d) for d in (1, -1, 2)})]
     for k in range(CH):
@@ -122,7 +124,8 @@
         rest = []
         for m in waiting:
             at = free.get(m["link"], 0.0)
-            if (at - now < LOOK or m["link"][0] == "x") and all(a in done for a in m["after"]):
+            look = LOOK if m["link"][0] != "x" else 1e3 if ("sel", last) in done else LOOK_X
+            if at - now < look and all(a in done for a in m["after"]):
                 end = max(now, at) + m["size"] * unit / rate[m["link"][0]]
                 free[m["link"]] = end
                 if m["name"] not in final:
@@ -136,15 +139,21 @@
     while flying or waiting or steps:
         flying.sort(key=lambda f: f[:2])
         ready = [step for step in steps if step[1] <= done]
-        if ready and (ready[0][0][0] in ("sel", "want") or not flying or flying[0][0] > now + 0.3):
+        ready.sort(key=lambda step: step[0][0] not in ("sel", "want"))
+        if ready and (ready[0][0][0] in ("sel", "want") or not flying or flying[0][0] > now + 0.3 or since >= EVENTS):
             name = ready[0][0]
             steps.remove(ready[0])
             order.append(name)
             now += COST[name[0]]
             done.add(name)
+            since = 0
+            if name == ("sel", last):
+                launch()
+                order.append(("drain",))
         elif flying:
             t, _, m = flying.pop(0)
-            now = max(now, t) + 0.05
+            now = max(now, t) + 0.1
+            since += 1
             order.append(("wait", m["name"]))
             done.add(m["name"])
         else:
@@ -207,8 +216,8 @@
 
     want_vmem[0] = jnp.zeros_like(want_vmem[0])
     want_vmem[0, :2, :SLOTS] = pairs_ref[...]
-    for n in range(IMG):
-        embedded[n] = jnp.dot(tokens_ref[n], embed_weight_ref[...], preferred_element_type=F32).astype(BF)
+    embedded[...] = jnp.dot(tokens_ref[...].reshape(IMG * TOK, D_ENC), embed_weight_ref[...],
+                            preferred_element_type=F32).astype(BF).reshape(IMG, TOK, D_DEC)
 
     pl.semaphore_wait(barrier, len(partners))
 
@@ -286,16 +295,13 @@
         for load in loads:
             load.wait()
 
-        def body(n, carry):
-            query_rows = jnp.dot(normed(embedded[n], gain_query_ref[...]), weights_vmem[0],
-                                 preferred_element_type=F32).astype(BF).astype(F32) * HEAD ** (-0.5)
+        query_rows = jnp.dot(normed(embedded[...].reshape(IMG * TOK, D_DEC), gain_query_ref[...]), weights_vmem[0],
+                             preferred_element_type=F32).astype(BF).astype(F32) * HEAD ** (-0.5)
+        for n in range(IMG):
             for p in range(PAIRS_OF_HEADS):
-                both = query_rows[:, p * 2 * HEAD:(p + 1) * 2 * HEAD]
+                both = query_rows[n * TOK:(n + 1) * TOK, p * 2 * HEAD:(p + 1) * 2 * HEAD]
                 stacked[n, p, :TOK] = jnp.where(lane < HEAD, both, 0.0).astype(BF)
                 stacked[n, p, TOK:] = jnp.where(lane >= HEAD, both, 0.0).astype(BF)
-            return carry
-
-        lax.fori_loop(0, IMG, body, 0)
 
     def project(k, g):
         slots = pl.ds(g * GROUP, GROUP)
@@ -327,6 +333,11 @@
             combined = embedded[image].astype(F32) + projected[b * TOK:(b + 1) * TOK]
             decoded_ref[slot] = jnp.where(slot < count_ref[0], combined, 0.0).astype(BF)
 
+    def drain():
+        for m in MESSAGES:
+            if m["link"][0] != "x":
+                descriptor(m["name"]).wait_send()
+
     def finish(names):
         def body(g, carry):
             for name in names:
@@ -338,12 +349,13 @@
         lax.fori_loop(0, SLOTS // GROUP, body, 0)
 
     run = dict(own=place_own, want=read_wants, sel=select, queries=make_queries, kv=project,
-               finish=finish,
+               finish=finish, drain=drain,
                start=lambda name: descriptor(name).start(), wait=lambda name: descriptor(name).wait_recv())
     for what, *which in ORDER:
         run[what](*which)
     for m in MESSAGES:
-        descriptor(m["name"]).wait_send()
+        if m["link"][0] == "x":
+            descriptor(m["name"]).wait_send()
 
 
 def decode(tokens, embed_weight, gain_query, gain_memory, query_weight, key_weight, value_weight, out_weight, pairs,

time: 110 us -> 109 us (level)
  no operation moved by 1% of the time
where the time goes in v5:
time: 109 us
  Pallas kernels  106 us (97%)
  local copies, waits for them, and re-layouts  2.38 us (2%)
    pallas_call x1, Pallas kernels, decode(): pl.pallas_call(decode_kernel, out_shape=pltpu.VMEM((SLOTS, TOK, D_DEC), B...  106 us
    unnamed x1, local copies, waits for them, and re-layouts  2.38 us

profile of v5, /device:TPU:1, one launch (start us, length us, event | category | flops | bytes accessed | tf_op | source)
XLA Modules:
  0.0 108.6 jit_solution(885631849833555259)
XLA Ops:
  0.7 105.6 %decode.1 = bf16[36,96,768]{2,1,0:T(8,128)(2,1)S(1)} custom-call(bf16[4,96,1024]{2,1,0:T(8,128)(2,1)} %tokens_ref.1, bf16[1024,768]{1,0:T(8,128)(2,1)} %embed_weight_ref.1, f32[768]{0:T(1024)} %gain_query_ref.1, f32[768]{0:T(1024)} %gain_memory_ref.1, bf16[768,768]{1,0:T(8,128)(2,1)} %query_weight_hbm.1, bf16[768,768]{1,0:T(8,128)(2,1)} %key_weight_hbm.1, ...), custom_call_target="tpu_custom_call" | custom-call | tf_op jit(solution)/shard_map/decode/pallas_call | solution.py:365
  106.3 2.4 %copy.12 = bf16[36,96,768]{2,1,0:T(8,128)(2,1)} copy(bf16[36,96,768]{2,1,0:T(8,128)(2,1)S(1)} %decode.1) | data formatting | bytes 10616832

commit v6 on v5

--- a/solution.py
+++ b/solution.py
@@ -21,6 +21,9 @@
 CH = 3
 CR = QR // CH
 KINDS = (1, 2, 2)
+EARLY = (3, 2, 2)
+FINE_Y = (True, True, False)
+FINE_Z = (False, False, False)
 GROUP = 12
 
 NY, NZ, NX = 4, 8, 4
@@ -39,48 +42,62 @@
 
     hz, hy = NZ // 2, NY // 2
 
-    def part(first, far, d):
-        return (first, 2) if not far else (first + (d == -1), 1)
+    def part(first, count, far, d):
+        if not far:
+            return (first, count)
+        upper = (count + 1) // 2
+        return (first, upper) if d == 1 else (first + upper, count - upper)
+
+    def all_of(legs, fine):
+        return legs if fine else {"all": [n for names in legs.values() for n in names]}
 
     for k in range(CH):
         quads = KINDS[k]
         own = ("own", k)
+        early = EARLY[k]
         along_z, along_y = {0: [own]}, {0: [own]}
         for s in range(1, hz + 1):
             for d in (1, -1):
-                name, images = ("az", k, d, s), part(0, s == hz, d)
-                add(name, ("z", d), quads * images[1], [("az", k, d, s - 1)] if s > 1 else [own],
-                    y=("one", 0), z=("one", -d * (s - 1)), l=images)
-                along_z.setdefault(hz if s == hz else -d * s, []).append(name)
+                name, images = ("az", k, d, s), part(0, early, s == hz, d)
+                if images[1]:
+                    add(name, ("z", d), quads * images[1], [("az", k, d, s - 1)] if s > 1 else [own],
+                        y=("one", 0), z=("one", -d * (s - 1)), l=images)
+                    along_z.setdefault(hz if s == hz else -d * s, []).append(name)
         for s in range(1, hy + 1):
             for d in (1, -1):
-                name, images = ("by", k, d, s), part(2, s == hy, d)
-                add(name, ("y", d), quads * images[1], [("by", k, d, s - 1)] if s > 1 else [own],
-                    y=("one", -d * (s - 1)), z=("one", 0), l=images)
-                along_y.setdefault(hy if s == hy else -d * s, []).append(name)
+                name, images = ("by", k, d, s), part(early, IMG - early, s == hy, d)
+                if images[1]:
+                    add(name, ("y", d), quads * images[1], [("by", k, d, s - 1)] if s > 1 else [own],
+                        y=("one", -d * (s - 1)), z=("one", 0), l=images)
+                    along_y.setdefault(hy if s == hy else -d * s, []).append(name)
         columns, planes = {}, {}
         for s in range(1, hy + 1):
             for d in (1, -1):
-                images = part(0, s == hy, d)
-                for at, arrived in along_z.items():
+                images = part(0, early, s == hy, d)
+                for at, arrived in all_of(along_z, FINE_Y[k]).items():
                     name = ("ay", k, d, s, at)
-                    add(name, ("y", d), quads * images[1], [("ay", k, d, s - 1, at)] if s > 1 else arrived,
-                        y=("one", -d * (s - 1)), z=("one", at), l=images)
-                    columns.setdefault(hy if s == hy else -d * s, []).append(name)
+                    if images[1]:
+                        add(name, ("y", d), quads * images[1] * (NZ if at == "all" else 1),
+                            [("ay", k, d, s - 1, at)] if s > 1 else arrived,
+                            y=("one", -d * (s - 1)), z=("all",) if at == "all" else ("one", at), l=images)
+                        columns.setdefault(hy if s == hy else -d * s, []).append(name)
         for s in range(1, hz + 1):
             for d in (1, -1):
-                images = part(2, s == hz, d)
-                for at, arrived in along_y.items():
+                images = part(early, IMG - early, s == hz, d)
+                for at, arrived in all_of(along_y, FINE_Z[k]).items():
                     name = ("bz", k, d, s, at)
-                    add(name, ("z", d), quads * images[1], [("bz", k, d, s - 1, at)] if s > 1 else arrived,
-                        y=("one", at), z=("one", -d * (s - 1)), l=images)
-                    planes.setdefault(hz if s == hz else -d * s, []).append(name)
+                    if images[1]:
+                        add(name, ("z", d), quads * images[1] * (NY if at == "all" else 1),
+                            [("bz", k, d, s - 1, at)] if s > 1 else arrived,
+                            y=("all",) if at == "all" else ("one", at), z=("one", -d * (s - 1)), l=images)
+                        planes.setdefault(hz if s == hz else -d * s, []).append(name)
         columns[0] = [n for at in along_z.values() for n in at]
         planes[0] = [n for at in along_y.values() for n in at]
         for at, arrived in columns.items():
-            add(("sa", k, at), ("c", 1), quads * 2 * NZ, arrived, y=("one", at), z=("all",), l=(0, 2))
+            add(("sa", k, at), ("c", 1), quads * early * NZ, arrived, y=("one", at), z=("all",), l=(0, early))
         for at, arrived in planes.items():
-            add(("sb", k, at), ("c", 1), quads * 2 * NY, arrived, y=("all",), z=("one", at), l=(2, 2))
+            add(("sb", k, at), ("c", 1), quads * (IMG - early) * NY, arrived, y=("all",), z=("one", at),
+                l=(early, IMG - early))
         for g in range(SLOTS // GROUP):
             for d in (1, -1):
                 if quads == 1:
@@ -93,14 +110,30 @@
     return messages
 
 
-LOOK = 2.0
+LOOK = 3.0
 LOOK_X = 2.5
 COST = {"sel": 1.0, "queries": 1.5, "kv": 1.2, "attend": 6.0, "want": 0.5}
 EVENTS = 8
 
 
+def with_drains(order, names, behind=48):
+    result, started = [], []
+    for n, entry in enumerate(order):
+        result.append(entry)
+        if entry[0] == "start" and entry[1] in names:
+            started.append((n, entry[1]))
+        elif entry[0] == "wait" and started and started[0][0] <= n - behind:
+            result.append(("sent", started.pop(0)[1]))
+        elif entry[0] == "drain":
+            result.pop()
+            result.extend(("sent", name) for _, name in started)
+            started = []
+    assert not started
+    return result
+
+
 def build_order(messages):
-    rate = {"x": 0.045, "y": 0.045, "z": 0.045, "c": 0.25}
+    rate = {"x": 0.055, "y": 0.045, "z": 0.045, "c": 0.25}
     unit = CR * QC * 2 / 1e6
     rank = {"wt": -1, "by": 0, "az": 0, "bz": 1, "ay": 1}
     waiting = sorted(messages, key=lambda m: (m["k"], rank.get(m["name"][0], 2)))
@@ -152,7 +185,7 @@
                 order.append(("drain",))
         elif flying:
             t, _, m = flying.pop(0)
-            now = max(now, t) + 0.1
+            now = max(now, t) + 0.15
             since += 1
             order.append(("wait", m["name"]))
             done.add(m["name"])
@@ -160,6 +193,7 @@
             now += 0.5
         launch()
     order.append(("finish", [("xd", last, d, 0) for d in (1, -1)]))
+    order = with_drains(order, {m["name"] for m in messages if m["link"][0] != "x"})
     return order, now + sum(COST[c] for c in ("kv", "attend")) * len(groups)
 
 
@@ -333,11 +367,6 @@
             combined = embedded[image].astype(F32) + projected[b * TOK:(b + 1) * TOK]
             decoded_ref[slot] = jnp.where(slot < count_ref[0], combined, 0.0).astype(BF)
 
-    def drain():
-        for m in MESSAGES:
-            if m["link"][0] != "x":
-                descriptor(m["name"]).wait_send()
-
     def finish(names):
         def body(g, carry):
             for name in names:
@@ -349,7 +378,7 @@
         lax.fori_loop(0, SLOTS // GROUP, body, 0)
 
     run = dict(own=place_own, want=read_wants, sel=select, queries=make_queries, kv=project,
-               finish=finish, drain=drain,
+               finish=finish, sent=lambda name: descriptor(name).wait_send(),
                start=lambda name: descriptor(name).start(), wait=lambda name: descriptor(name).wait_recv())
     for what, *which in ORDER:
         run[what](*which)

time: 109 us -> 108 us (level)
  no operation moved by 1% of the time
where the time goes in v6:
time: 108 us
  Pallas kernels  105 us (97%)
  local copies, waits for them, and re-layouts  2.38 us (2%)
    pallas_call x1, Pallas kernels, decode(): pl.pallas_call(decode_kernel, out_shape=pltpu.VMEM((SLOTS, TOK, D_DEC), B...  105 us
    unnamed x1, local copies, waits for them, and re-layouts  2.38 us

profile of v6, /device:TPU:1, one launch (start us, length us, event | category | flops | bytes accessed | tf_op | source)
XLA Modules:
  0.0 107.9 jit_solution(17078958237734892956)
XLA Ops:
  0.7 104.8 %decode.1 = bf16[36,96,768]{2,1,0:T(8,128)(2,1)S(1)} custom-call(bf16[4,96,1024]{2,1,0:T(8,128)(2,1)} %tokens_ref.1, bf16[1024,768]{1,0:T(8,128)(2,1)} %embed_weight_ref.1, f32[768]{0:T(1024)} %gain_query_ref.1, f32[768]{0:T(1024)} %gain_memory_ref.1, bf16[768,768]{1,0:T(8,128)(2,1)} %query_weight_hbm.1, bf16[768,768]{1,0:T(8,128)(2,1)} %key_weight_hbm.1, ...), custom_call_target="tpu_custom_call" | custom-call | tf_op jit(solution)/shard_map/decode/pallas_call | solution.py:394
  105.5 2.4 %copy.12 = bf16[36,96,768]{2,1,0:T(8,128)(2,1)} copy(bf16[36,96,768]{2,1,0:T(8,128)(2,1)S(1)} %decode.1) | data formatting | bytes 10616832

commit v7 on v6

--- a/solution.py
+++ b/solution.py
@@ -116,24 +116,8 @@
 EVENTS = 8
 
 
-def with_drains(order, names, behind=48):
-    result, started = [], []
-    for n, entry in enumerate(order):
-        result.append(entry)
-        if entry[0] == "start" and entry[1] in names:
-            started.append((n, entry[1]))
-        elif entry[0] == "wait" and started and started[0][0] <= n - behind:
-            result.append(("sent", started.pop(0)[1]))
-        elif entry[0] == "drain":
-            result.pop()
-            result.extend(("sent", name) for _, name in started)
-            started = []
-    assert not started
-    return result
-
-
 def build_order(messages):
-    rate = {"x": 0.055, "y": 0.045, "z": 0.045, "c": 0.25}
+    rate = {"x": 0.045, "y": 0.045, "z": 0.045, "c": 0.25}
     unit = CR * QC * 2 / 1e6
     rank = {"wt": -1, "by": 0, "az": 0, "bz": 1, "ay": 1}
     waiting = sorted(messages, key=lambda m: (m["k"], rank.get(m["name"][0], 2)))
@@ -193,7 +177,6 @@
             now += 0.5
         launch()
     order.append(("finish", [("xd", last, d, 0) for d in (1, -1)]))
-    order = with_drains(order, {m["name"] for m in messages if m["link"][0] != "x"})
     return order, now + sum(COST[c] for c in ("kv", "attend")) * len(groups)
 
 
@@ -367,6 +350,11 @@
             combined = embedded[image].astype(F32) + projected[b * TOK:(b + 1) * TOK]
             decoded_ref[slot] = jnp.where(slot < count_ref[0], combined, 0.0).astype(BF)
 
+    def drain():
+        for m in MESSAGES:
+            if m["link"][0] != "x":
+                descriptor(m["name"]).wait_send()
+
     def finish(names):
         def body(g, carry):
             for name in names:
@@ -378,7 +366,7 @@
         lax.fori_loop(0, SLOTS // GROUP, body, 0)
 
     run = dict(own=place_own, want=read_wants, sel=select, queries=make_queries, kv=project,
-               finish=finish, sent=lambda name: descriptor(name).wait_send(),
+               finish=finish, drain=drain,
                start=lambda name: descriptor(name).start(), wait=lambda name: descriptor(name).wait_recv())
     for what, *which in ORDER:
         run[what](*which)

time: 108 us -> 107 us (level)
  Pallas kernels: 105 us -> 103 us
    pallas_call x1, Pallas kernels: 105 us -> 103 us  [decode(): pl.pallas_call(decode_kernel, out_shape=pltpu.VMEM((SLOTS, TOK, D_DEC), B...]
where the time goes in v7:
time: 107 us; the launch traced here: 106 us
  Pallas kernels  103 us (96%)
  local copies, waits for them, and re-layouts  2.38 us (2%)
    pallas_call x1, Pallas kernels, decode(): pl.pallas_call(decode_kernel, out_shape=pltpu.VMEM((SLOTS, TOK, D_DEC), B...  103 us
    unnamed x1, local copies, waits for them, and re-layouts  2.38 us

profile of v7, /device:TPU:1, one launch (start us, length us, event | category | flops | bytes accessed | tf_op | source)
XLA Modules:
  0.0 106.4 jit_solution(10435262615842871642)
XLA Ops:
  0.7 103.4 %decode.1 = bf16[36,96,768]{2,1,0:T(8,128)(2,1)S(1)} custom-call(bf16[4,96,1024]{2,1,0:T(8,128)(2,1)} %tokens_ref.1, bf16[1024,768]{1,0:T(8,128)(2,1)} %embed_weight_ref.1, f32[768]{0:T(1024)} %gain_query_ref.1, f32[768]{0:T(1024)} %gain_memory_ref.1, bf16[768,768]{1,0:T(8,128)(2,1)} %query_weight_hbm.1, bf16[768,768]{1,0:T(8,128)(2,1)} %key_weight_hbm.1, ...), custom_call_target="tpu_custom_call" | custom-call | tf_op jit(solution)/shard_map/decode/pallas_call | solution.py:382
  104.1 2.4 %copy.12 = bf16[36,96,768]{2,1,0:T(8,128)(2,1)} copy(bf16[36,96,768]{2,1,0:T(8,128)(2,1)S(1)} %decode.1) | data formatting | bytes 10616832
